TPU v7x, 512 devices: a whole 4x8x8 slice. The times are simulated.
512 devices in a mesh: gy: 32 (over z, y_lo), gx: 16 (over y_hi, x, core).
Axes of the slice: x: 4, y: 8 (y_hi: 2, y_lo: 4; y = y_hi * 4 + y_lo), z: 8, core: 2. Of those that a mesh axis runs over, the one named last changes fastest.
Arguments:
- tokens: bfloat16 [256, 256, 384], P('gy', 'gx'), may hold values from -6 to 6
- norm_gain: float32 [384], replicated, may hold values from 0.25 to 1.75
- norm_bias: float32 [384], replicated, may hold values from -1.5 to 1.5
- w_in: bfloat16 [384, 1536], replicated, may hold values from -0.3125 to 0.3125
- conv_taps: float32 [9, 768], replicated, may hold values from -3.5 to 3.5
- conv_bias: float32 [768], replicated, may hold values from -1.5 to 1.5
- w_x: bfloat16 [4, 768, 40], replicated, may hold values from -0.21875 to 0.21875
- w_dt: bfloat16 [4, 24, 768], replicated, may hold values from -1.25 to 1.25
- dt_bias: float32 [4, 768], replicated, may hold values from -1 to 0.5
- a_log: float32 [4, 8, 768], replicated, may hold values from -10 to -2
- d_skip: float32 [4, 768], replicated, may hold values from 0.5 to 1.5
- out_gain: float32 [768], replicated, may hold values from 0.25 to 1.75
- out_bias: float32 [768], replicated, may hold values from -1.5 to 1.5
- w_out: bfloat16 [768, 384], replicated, may hold values from -0.21875 to 0.21875
Outputs:
- mixed: bfloat16 [256, 256, 384], P('gy', 'gx')
All inputs are finite; a program needn't handle non-finite values.
Results may differ from a plain program's by a relative error of at most 0.0055.
The roundings to bfloat16 on the way count: a program that leaves them out, or rounds other values in their place, can miss the bound.
Values may be sent and summed in bfloat16 or wider, within the bound.
A program may use at most 192 MiB of HBM per device.

v0:
```python
import jax
import jax.numpy as jnp
from jax import lax
from jax.sharding import PartitionSpec as P


def prefix(shard, axis, combine, identity, reverse):
    size, index = (lax.axis_size(axis), lax.axis_index(axis))
    everything = jax.tree.map(lambda part: lax.all_gather(part, axis), shard)
    start = jax.tree.map(
        lambda part, zero: jnp.broadcast_to(jnp.asarray(zero, part.dtype), part.shape),
        shard,
        identity,
    )

    def lap(k, before):
        at = size - 1 - k if reverse else k
        reached = at > index if reverse else at < index
        new = combine(before, jax.tree.map(lambda part: part[at], everything))
        return jax.tree.map(lambda a, b: jnp.where(reached, a, b), new, before)

    return lax.fori_loop(0, size, lap, start)


def extended(cells, sides, width):
    for axis, dim in sides:
        count = lax.axis_size(axis)
        ends = count - 1
        head = lax.slice_in_dim(cells, 0, width, axis=dim)
        tail = lax.slice_in_dim(cells, cells.shape[dim] - width, cells.shape[dim], axis=dim)
        cells = jnp.concatenate(
            [
                lax.ppermute(tail, axis, [(i, (i + 1) % count) for i in range(ends)]),
                cells,
                lax.ppermute(head, axis, [((i + 1) % count, i) for i in range(ends)]),
            ],
            axis=dim,
        )
    return cells


def layer_norm(values, gain, bias):
    mean = jnp.mean(values, axis=-1, keepdims=True)
    centred = values - mean
    spread = jnp.mean(centred * centred, axis=-1, keepdims=True)
    return centred * lax.rsqrt(spread + 1e-05) * gain + bias


def orient(array, direction):
    if direction < 2:
        array = jnp.transpose(array, (1, 0, 2))
    if direction % 2 == 1:
        array = array[::-1]
    return array


def unorient(array, direction):
    if direction % 2 == 1:
        array = array[::-1]
    if direction < 2:
        array = jnp.transpose(array, (1, 0, 2))
    return array


def local_scan(drive, steps, in_maps, out_maps, rates):

    def advance(state, items):
        driven, step, in_map, out_map = items
        decay = jnp.exp(step[None] * rates[:, None, :])
        state = decay * state + in_map.T[:, :, None] * driven[None]
        return (state, jnp.sum(out_map.T[:, :, None] * state, axis=0))

    start = jnp.zeros((rates.shape[0], drive.shape[1], drive.shape[2]), jnp.float32)
    final, outputs = lax.scan(advance, start, (drive, steps, in_maps, out_maps))
    return (outputs, final)


def chain_decay(earlier, later):
    return (earlier[0] * later[0], later[0] * earlier[1] + later[1])


def carry_decays(pair, direction):
    identity = (jnp.ones_like(pair[0]), jnp.zeros_like(pair[1]))
    if direction == 0:
        return prefix(pair, "gx", chain_decay, identity, False)[1]
    if direction == 1:
        return prefix(pair, "gx", chain_decay, identity, True)[1]
    if direction == 2:
        return prefix(pair, "gy", chain_decay, identity, False)[1]
    return prefix(pair, "gy", chain_decay, identity, True)[1]


def shards(
    tokens,
    norm_gain,
    norm_bias,
    w_in,
    conv_taps,
    conv_bias,
    w_x,
    w_dt,
    dt_bias,
    a_log,
    d_skip,
    out_gain,
    out_bias,
    w_out,
):
    height, width, chans = tokens.shape
    inner_width = w_in.shape[1] // 2
    rank = w_dt.shape[1]
    states = a_log.shape[1]
    token_float = tokens.astype(jnp.float32)
    normed = layer_norm(token_float, norm_gain, norm_bias).astype(jnp.bfloat16)
    projected = jnp.dot(normed.reshape(-1, chans), w_in, preferred_element_type=jnp.float32).astype(
        jnp.bfloat16
    )
    projected = projected.reshape(height, width, 2 * inner_width)
    gate = projected[..., inner_width:]
    padded = extended(projected[..., :inner_width], (("gy", 0), ("gx", 1)), 1)
    conv_sum = jnp.zeros((height, width, inner_width), jnp.float32) + conv_bias
    for row_tap in range(3):
        for col_tap in range(3):
            conv_sum = (
                conv_sum
                + padded[row_tap : row_tap + height, col_tap : col_tap + width]
                * conv_taps[3 * row_tap + col_tap]
            )
    conved = jax.nn.silu(conv_sum).astype(jnp.bfloat16)
    conved_flat = conved.reshape(-1, inner_width)
    conved_float = conved.astype(jnp.float32)
    summed = jnp.zeros((height, width, inner_width), jnp.float32)
    for direction in range(4):
        proj = jnp.dot(conved_flat, w_x[direction], preferred_element_type=jnp.float32)
        low = proj[:, :rank].astype(jnp.bfloat16)
        in_maps = orient(proj[:, rank : rank + states].reshape(height, width, states), direction)
        out_maps = orient(proj[:, rank + states :].reshape(height, width, states), direction)
        step_flat = jax.nn.softplus(
            jnp.dot(low, w_dt[direction], preferred_element_type=jnp.float32) + dt_bias[direction]
        )
        step_grid = step_flat.reshape(height, width, inner_width)
        steps = orient(step_grid, direction)
        drive = orient(step_grid * conved_float, direction)
        rates = -jnp.exp(a_log[direction])
        outputs, final = local_scan(drive, steps, in_maps, out_maps, rates)
        elapsed = jnp.cumsum(steps, axis=0)
        total_decay = jnp.exp(rates[:, None, :] * elapsed[-1][None])
        incoming = carry_decays((total_decay, final), direction)
        for state_index in range(states):
            outputs = (
                outputs
                + out_maps[..., state_index][..., None]
                * jnp.exp(rates[state_index] * elapsed)
                * incoming[state_index][None]
            )
        summed = summed + unorient(outputs, direction) + d_skip[direction] * conved_float
    gated = (layer_norm(summed, out_gain, out_bias) * jax.nn.silu(gate.astype(jnp.float32))).astype(
        jnp.bfloat16
    )
    result = token_float + jnp.dot(
        gated.reshape(-1, inner_width), w_out, preferred_element_type=jnp.float32
    ).reshape(height, width, chans)
    return result.astype(jnp.bfloat16)


def solution(mesh):
    placed = (P("gy", "gx", None), P(), P(), P(), P(), P(), P(), P(), P(), P(), P(), P(), P(), P())
    return jax.shard_map(
        shards, mesh=mesh, in_specs=placed, out_specs=P("gy", "gx", None), check_vma=False
    )
```

profile of v0, /device:TPU:1, one launch (start us, length us, event | category | flops | bytes accessed | tf_op | source)
XLA Modules:
  0.0 1555.3 jit_solution(1925314627477764077)
XLA Ops:
  10.3 4.2 collective-permute-start
  17.4 2.5 collective-permute-done.1
  20.0 5.1 collective-permute-start.2
  25.1 2.9 collective-permute-start.3
  28.1 2.2 collective-permute-done.3
  34.2 1.9 fusion.14
  36.1 16.5 %while.112 = (s32[]{:T(128)}, f32[8,8,768]{2,1,0:T(8,128)S(1)}, f32[16,8,768]{2,1,0:T(8,128)S(1)}, f32[16,8,768]{2,1,0:T(8,128)}, f32[8,768]{1,0:T(8,128)S(1)}, ...) while((s32[]{:T(128)}, f32[8,8,768]{2,1,0:T(8,128)S(1)}, ...), condition=%wide.region_4.5_spmd.clone, body=%wide.region_2.4_spmd.clone.sunk | while | flops 337923 | bytes 641659 | solution.py:74
  56.5 16.8 %while.114 = (s32[]{:T(128)}, f32[8,8,768]{2,1,0:T(8,128)S(1)}, f32[16,8,768]{2,1,0:T(8,128)S(1)}, f32[16,8,768]{2,1,0:T(8,128)S(1)}, f32[8,768]{1,0:T(8,128)}, ...) while((s32[]{:T(128)}, f32[8,8,768]{2,1,0:T(8,128)S(1)}, ...), condition=%wide.region_10.11_spmd.clone, body=%wide.region_8.10_spmd.clone.sunk | while | flops 337923 | bytes 641659 | solution.py:74
  74.1 3.8 fusion.70
  78.0 1.5 multiply_exponential_fusion.2
  80.5 30.6 %while.116 = (s32[]{:T(128)}, f32[8,16,768]{2,1,0:T(8,128)S(1)}, f32[8,16,768]{2,0,1:T(8,128)S(1)}, f32[8,16,768]{2,1,0:T(8,128)}, f32[8,768]{1,0:T(8,128)S(1)},...) while((s32[]{:T(128)}, f32[8,16,768]{2,1,0:T(8,128)S(1)}, ...), condition=%wide.region_16.17_spmd.clone, body=%wide.region_14.16_spmd.clone.sunk | while | flops 675843 | bytes 1453183 | solution.py:74
  82.6 1.7 dynamic_update_slice.26
  86.4 1.7 dynamic_update_slice.26
  90.2 1.7 dynamic_update_slice.26
  94.1 1.7 dynamic_update_slice.26
  97.9 1.7 dynamic_update_slice.26
  101.7 1.7 dynamic_update_slice.26
  105.5 1.7 dynamic_update_slice.26
  109.3 1.7 dynamic_update_slice.26
  114.5 16.7 %while.118 = (s32[]{:T(128)}, f32[8,16,768]{2,1,0:T(8,128)S(1)}, f32[8,16,768]{2,0,1:T(8,128)S(1)}, f32[8,16,768]{2,0,1:T(8,128)S(1)}, f32[8,768]{1,0:T(8,128)S(...) while((s32[]{:T(128)}, f32[8,16,768]{2,1,0:T(8,128)S(1)}, ...), condition=%wide.region_22.23_spmd.clone, body=%wide.region_20.22_spmd.clone.sunk | while | flops 675843 | bytes 1551487 | solution.py:74
  114.9 1.7 dynamic_update_slice.27
  117.0 1.7 dynamic_update_slice.27
  119.1 1.7 dynamic_update_slice.27
  121.1 1.7 dynamic_update_slice.27
  123.2 1.7 dynamic_update_slice.27
  125.3 1.7 dynamic_update_slice.27
  127.4 1.7 dynamic_update_slice.27
  129.5 1.7 dynamic_update_slice.27
  133.6 1.5 slice_reduce_fusion.38
  135.1 1.8 slice_reduce_fusion.7
  156.0 60.3 %all-gather.13.cloned.1.call-done = f32[16,8,8,768]{3,2,1,0:T(8,128)} async-done(((f32[1,8,8,768]{3,2,1,0:T(8,128)}), f32[16,8,8,768]{3,2,1,0:T(8,128)}) %all-gather.13.cloned.1.call-update) | async-done | bytes 3145744 | tf_op jit(solution)/shard_map/all_gather | solution.py:9
  216.3 19.3 %while.113 = (s32[]{:T(128)}, f32[8,8,768]{2,1,0:T(8,128)S(1)}, s32[]{:T(128)}, f32[16,8,8,768]{3,2,1,0:T(8,128)}, f32[16,8,8,768]{3,2,1,0:T(8,128)}, /*index=5*/s32[]{:T(128)}, s32[]{:T(128)}) while((s32[]{:T(128)}, f32[8,8,768]{2,1,0:T(8,128)S(1)}, s32[]{:T(128)}, f32[16,8,8,768]{3,2,1,0:T(8,128)}, f32[16,8,8,768]{3,2,1,0:T(8,128)}, ...), condition=%wide.region_7.8_spmd.clone, body=%wide.region_6.7_spmd.clone.sunk | while | flops 196612 | bytes 786533 | solution.py:22
  236.5 54.5 %all-gather.23.cloned.1.call-done = f32[128,8,768]{2,1,0:T(8,128)} async-done(((f32[8,8,768]{2,1,0:T(8,128)}), f32[128,8,768]{2,1,0:T(8,128)}) %all-gather.23.cloned.1.call-update) | async-done | bytes 3145744 | tf_op jit(solution)/shard_map/all_gather | solution.py:9
  291.0 74.5 %all-gather.15.cloned.1.call-done = f32[16,8,8,768]{3,2,1,0:T(8,128)} async-done(((f32[1,8,8,768]{3,2,1,0:T(8,128)}), f32[16,8,8,768]{3,2,1,0:T(8,128)}) %all-gather.15.cloned.1.call-update) | async-done | bytes 3145744 | tf_op jit(solution)/shard_map/all_gather | solution.py:9
  365.5 19.4 %while.115 = (s32[]{:T(128)}, f32[8,8,768]{2,1,0:T(8,128)S(1)}, s32[]{:T(128)}, f32[16,8,8,768]{3,2,1,0:T(8,128)}, f32[16,8,8,768]{3,2,1,0:T(8,128)}, /*index=5*/s32[]{:T(128)}, s32[]{:T(128)}, s32[]{:T(128)}, s32[]{:T(128)}) while((s32[]{:T(128)}, f32[8,8,768]{2,1,0:T(8,128)S(1)}, s32[]{:T(128)}, f32[16,8,8,768]{3,2,1,0:T(8,128)}, ...), condition=%wide.region_13.14_spmd.clone, body=%wide.region_12.13_spmd.clone.sunk | while | flops 196616 | bytes 786595 | solution.py:22
  386.5 260.9 %all-gather.25.cloned.1.call-done = f32[256,16,768]{2,1,0:T(8,128)} async-done(((f32[8,16,768]{2,1,0:T(8,128)}), f32[256,16,768]{2,1,0:T(8,128)}) %all-gather.25.cloned.1.call-update) | async-done | bytes 12582928 | tf_op jit(solution)/shard_map/all_gather | solution.py:9
  647.4 281.2 %all-gather.17.cloned.1.call-done = f32[32,8,16,768]{3,2,1,0:T(8,128)} async-done(((f32[1,8,16,768]{3,2,1,0:T(8,128)}), f32[32,8,16,768]{3,2,1,0:T(8,128)}) %all-gather.17.cloned.1.call-update) | async-done | bytes 12582928 | tf_op jit(solution)/shard_map/all_gather | solution.py:9
  928.6 47.5 %while.117 = (s32[]{:T(128)}, f32[8,16,768]{2,1,0:T(8,128)S(1)}, s32[]{:T(128)}, f32[32,8,16,768]{3,2,1,0:T(8,128)}, f32[32,8,16,768]{3,2,1,0:T(8,128)}, /*index=5*/s32[]{:T(128)}, s32[]{:T(128)}) while((s32[]{:T(128)}, f32[8,16,768]{2,1,0:T(8,128)S(1)}, s32[]{:T(128)}, f32[32,8,16,768]{3,2,1,0:T(8,128)}, ...), condition=%wide.region_19.20_spmd.clone, body=%wide.region_18.19_spmd.clone.sunk | while | flops 393220 | bytes 1572965 | solution.py:22
  940.4 1.5 fusion.84
  953.8 1.5 fusion.84
  958.3 1.5 fusion.84
  968.7 1.5 fusion.84
  976.8 233.1 %all-gather.27.cloned.1.call-done = f32[256,16,768]{2,1,0:T(8,128)} async-done(((f32[8,16,768]{2,1,0:T(8,128)}), f32[256,16,768]{2,1,0:T(8,128)}) %all-gather.27.cloned.1.call-update) | async-done | bytes 12582928 | tf_op jit(solution)/shard_map/all_gather | solution.py:9
  1209.9 281.3 %all-gather.19.cloned.1.call-done = f32[32,8,16,768]{3,2,1,0:T(8,128)} async-done(((f32[1,8,16,768]{3,2,1,0:T(8,128)}), f32[32,8,16,768]{3,2,1,0:T(8,128)}) %all-gather.19.cloned.1.call-update) | async-done | bytes 12582928 | tf_op jit(solution)/shard_map/all_gather | solution.py:9
  1491.4 47.7 %while.119 = (s32[]{:T(128)}, f32[8,16,768]{2,1,0:T(8,128)S(1)}, s32[]{:T(128)}, f32[32,8,16,768]{3,2,1,0:T(8,128)}, f32[32,8,16,768]{3,2,1,0:T(8,128)}, /*index=5*/s32[]{:T(128)}, s32[]{:T(128)}, s32[]{:T(128)}, s32[]{:T(128)}) while((s32[]{:T(128)}, f32[8,16,768]{2,1,0:T(8,128)S(1)}, s32[]{:T(128)}, ...), condition=%wide.region_25.26_spmd.clone, body=%wide.region_24.25_spmd.clone.sunk | while | flops 393224 | bytes 1573027 | solution.py:22
  1491.4 1.6 fusion.85
  1540.2 3.9 fusion.60
  1546.5 2.0 fusion.8
  (658 shorter events, 222.0 us)
Async XLA Ops:
  6.5 21.5 %copy-start.43 = (f32[4,768]{1,0:T(4,128)S(1)}, f32[4,768]{1,0:T(4,128)}, u32[]{:S(2)}) copy-start(f32[4,768]{1,0:T(4,128)} %param.38) | copy-start | bytes 36868
  6.5 24.1 %copy-start.48 = (f32[768]{0:T(1024)S(1)}, f32[768]{0:T(1024)}, u32[]{:S(2)}) copy-start(f32[768]{0:T(1024)} %param.35) | copy-start | bytes 9220
  6.5 149.5 %all-gather.21.cloned.1.call-start = ((), (), s32[]{:S(2)}) async-start(), calls=%async_computation.4 | async-start | bytes 3342336 | tf_op jit(solution)/shard_map/all_gather | solution.py:9
  10.2 21.1 %copy-start.21 = (bf16[4,768,40]{1,2,0:T(8,128)(2,1)S(1)}, bf16[4,768,40]{1,2,0:T(8,128)(2,1)}, u32[]{:S(2)}) copy-start(bf16[4,768,40]{1,2,0:T(8,128)(2,1)} %param.36) | copy-start | bytes 737284
  10.3 7.2 collective-permute-start
  14.5 5.5 collective-permute-start.1
  20.0 8.0 collective-permute-start.2
  25.1 5.1 collective-permute-start.3
  53.3 163.0 %all-gather.13.cloned.1.call-start = ((), (), s32[]{:S(2)}) async-start(), calls=%async_computation | async-start | bytes 3342336 | tf_op jit(solution)/shard_map/all_gather | solution.py:9
  56.4 24.0 %copy-start.15 = (f32[8,768]{1,0:T(8,128)S(1)}, f32[8,768]{1,0:T(8,128)}, u32[]{:S(2)}) copy-start(f32[8,768]{1,0:T(8,128)} %get-tuple-element.1669) | copy-start | bytes 73732
  56.4 234.5 %all-gather.23.cloned.1.call-start = ((), (), s32[]{:S(2)}) async-start(), calls=%async_computation.5 | async-start | bytes 3342336 | tf_op jit(solution)/shard_map/all_gather | solution.py:9
  74.1 291.4 %all-gather.15.cloned.1.call-start = ((), (), s32[]{:S(2)}) async-start(), calls=%async_computation.1 | async-start | bytes 3342336 | tf_op jit(solution)/shard_map/all_gather | solution.py:9
  79.5 567.9 %all-gather.25.cloned.1.call-start = ((), (), s32[]{:S(2)}) async-start(), calls=%async_computation.6 | async-start | bytes 12976128 | tf_op jit(solution)/shard_map/all_gather | solution.py:9
  80.5 31.4 %copy-start.6 = (f32[8,16,768]{2,0,1:T(8,128)S(1)}, f32[8,16,768]{2,0,1:T(8,128)}, u32[]{:S(2)}) copy-start(f32[8,16,768]{2,0,1:T(8,128)} %get-tuple-element.1166) | copy-start | bytes 1179652
  111.8 816.8 %all-gather.17.cloned.1.call-start = ((), (), s32[]{:S(2)}) async-start(), calls=%async_computation.2 | async-start | bytes 12976128 | tf_op jit(solution)/shard_map/all_gather | solution.py:9
  113.2 1096.8 %all-gather.27.cloned.1.call-start = ((), (), s32[]{:S(2)}) async-start(), calls=%async_computation.7 | async-start | bytes 12976128 | tf_op jit(solution)/shard_map/all_gather | solution.py:9
  132.1 1359.1 %all-gather.19.cloned.1.call-start = ((), (), s32[]{:S(2)}) async-start(), calls=%async_computation.3 | async-start | bytes 12976128 | tf_op jit(solution)/shard_map/all_gather | solution.py:9
  235.6 149.3 %copy-start.18 = (f32[16,8,768]{2,1,0:T(8,128)S(1)}, f32[16,8,768]{2,1,0:T(8,128)}, u32[]{:S(2)}) copy-start(f32[16,8,768]{2,1,0:T(8,128)} %copy-done.17) | copy-start | bytes 1179652
  235.6 149.3 %copy-start.20 = (f32[16,8,768]{2,1,0:T(8,128)S(1)}, f32[16,8,768]{2,1,0:T(8,128)}, u32[]{:S(2)}) copy-start(f32[16,8,768]{2,1,0:T(8,128)} %copy-done.19) | copy-start | bytes 1179652
  235.6 149.3 %copy-start.44 = (f32[16,8]{1,0:T(8,128)S(1)}, f32[16,8]{1,0:T(8,128)}, u32[]{:S(2)}) copy-start(f32[16,8]{1,0:T(8,128)} %copy.237) | copy-start | bytes 1540
  235.6 149.3 %copy-start.45 = (f32[16,8]{1,0:T(8,128)S(1)}, f32[16,8]{1,0:T(8,128)}, u32[]{:S(2)}) copy-start(f32[16,8]{1,0:T(8,128)} %copy.238) | copy-start | bytes 1540
  235.7 149.3 %copy-start.46 = (f32[16,8]{1,0:T(8,128)S(1)}, f32[16,8]{1,0:T(8,128)}, u32[]{:S(2)}) copy-start(f32[16,8]{1,0:T(8,128)} %copy.239) | copy-start | bytes 1540
  235.7 149.3 %copy-start.47 = (f32[16,8]{1,0:T(8,128)S(1)}, f32[16,8]{1,0:T(8,128)}, u32[]{:S(2)}) copy-start(f32[16,8]{1,0:T(8,128)} %copy.240) | copy-start | bytes 1540
  235.7 149.3 %copy-start.49 = (f32[768]{0:T(1024)S(1)}, f32[768]{0:T(1024)}, u32[]{:S(2)}) copy-start(f32[768]{0:T(1024)} %get-tuple-element.1228) | copy-start | bytes 9220
  235.7 149.3 %copy-start.50 = (f32[768]{0:T(1024)S(1)}, f32[768]{0:T(1024)}, u32[]{:S(2)}) copy-start(f32[768]{0:T(1024)} %get-tuple-element.1229) | copy-start | bytes 9220
  235.7 149.3 %copy-start.51 = (f32[768]{0:T(1024)S(1)}, f32[768]{0:T(1024)}, u32[]{:S(2)}) copy-start(f32[768]{0:T(1024)} %get-tuple-element.1230) | copy-start | bytes 9220
  235.7 149.3 %copy-start.52 = (f32[768]{0:T(1024)S(1)}, f32[768]{0:T(1024)}, u32[]{:S(2)}) copy-start(f32[768]{0:T(1024)} %get-tuple-element.1231) | copy-start | bytes 9220
  235.7 149.3 %copy-start.53 = (f32[768]{0:T(1024)S(1)}, f32[768]{0:T(1024)}, u32[]{:S(2)}) copy-start(f32[768]{0:T(1024)} %get-tuple-element.1232) | copy-start | bytes 9220
  235.7 149.3 %copy-start.54 = (f32[768]{0:T(1024)S(1)}, f32[768]{0:T(1024)}, u32[]{:S(2)}) copy-start(f32[768]{0:T(1024)} %get-tuple-element.1233) | copy-start | bytes 9220
  235.7 149.3 %copy-start.55 = (f32[768]{0:T(1024)S(1)}, f32[768]{0:T(1024)}, u32[]{:S(2)}) copy-start(f32[768]{0:T(1024)} %get-tuple-element.1234) | copy-start | bytes 9220
  235.8 149.3 %copy-start.56 = (f32[768]{0:T(1024)S(1)}, f32[768]{0:T(1024)}, u32[]{:S(2)}) copy-start(f32[768]{0:T(1024)} %get-tuple-element.1235) | copy-start | bytes 9220
  1491.2 47.9 %copy-start.11 = (f32[8,16,768]{2,0,1:T(8,128)S(1)}, f32[8,16,768]{2,0,1:T(8,128)}, u32[]{:S(2)}) copy-start(f32[8,16,768]{2,0,1:T(8,128)} %copy-done.10) | copy-start | bytes 1179652
  1491.2 47.9 %copy-start.26 = (f32[8,16]{0,1:T(8,128)S(1)}, f32[8,16]{0,1:T(8,128)}, u32[]{:S(2)}) copy-start(f32[8,16]{0,1:T(8,128)} %copy.261) | copy-start | bytes 1540
  1491.2 47.9 %copy-start.27 = (f32[8,16]{0,1:T(8,128)S(1)}, f32[8,16]{0,1:T(8,128)}, u32[]{:S(2)}) copy-start(f32[8,16]{0,1:T(8,128)} %copy.263) | copy-start | bytes 1540
  1491.2 47.9 %copy-start.28 = (f32[8,16]{0,1:T(8,128)S(1)}, f32[8,16]{0,1:T(8,128)}, u32[]{:S(2)}) copy-start(f32[8,16]{0,1:T(8,128)} %copy.264) | copy-start | bytes 1540
  1491.2 47.9 %copy-start.29 = (f32[8,16]{0,1:T(8,128)S(1)}, f32[8,16]{0,1:T(8,128)}, u32[]{:S(2)}) copy-start(f32[8,16]{0,1:T(8,128)} %copy.265) | copy-start | bytes 1540
  1491.2 47.9 %copy-start.30 = (f32[8,16]{0,1:T(8,128)S(1)}, f32[8,16]{0,1:T(8,128)}, u32[]{:S(2)}) copy-start(f32[8,16]{0,1:T(8,128)} %copy.266) | copy-start | bytes 1540
  1491.3 47.9 %copy-start.31 = (f32[8,16]{0,1:T(8,128)S(1)}, f32[8,16]{0,1:T(8,128)}, u32[]{:S(2)}) copy-start(f32[8,16]{0,1:T(8,128)} %copy.267) | copy-start | bytes 1540
  1491.3 47.9 %copy-start.32 = (f32[8,16]{0,1:T(8,128)S(1)}, f32[8,16]{0,1:T(8,128)}, u32[]{:S(2)}) copy-start(f32[8,16]{0,1:T(8,128)} %copy.268) | copy-start | bytes 1540
  1491.3 47.9 %copy-start.33 = (f32[8,16]{0,1:T(8,128)S(1)}, f32[8,16]{0,1:T(8,128)}, u32[]{:S(2)}) copy-start(f32[8,16]{0,1:T(8,128)} %copy.269) | copy-start | bytes 1540
  1491.3 47.9 %copy-start.34 = (f32[768]{0:T(1024)S(1)}, f32[768]{0:T(1024)}, u32[]{:S(2)}) copy-start(f32[768]{0:T(1024)} %get-tuple-element.982) | copy-start | bytes 9220
  1491.3 47.9 %copy-start.35 = (f32[768]{0:T(1024)S(1)}, f32[768]{0:T(1024)}, u32[]{:S(2)}) copy-start(f32[768]{0:T(1024)} %get-tuple-element.983) | copy-start | bytes 9220
  1491.3 47.9 %copy-start.36 = (f32[768]{0:T(1024)S(1)}, f32[768]{0:T(1024)}, u32[]{:S(2)}) copy-start(f32[768]{0:T(1024)} %get-tuple-element.984) | copy-start | bytes 9220
  1491.3 47.9 %copy-start.37 = (f32[768]{0:T(1024)S(1)}, f32[768]{0:T(1024)}, u32[]{:S(2)}) copy-start(f32[768]{0:T(1024)} %get-tuple-element.985) | copy-start | bytes 9220
  1491.3 47.9 %copy-start.38 = (f32[768]{0:T(1024)S(1)}, f32[768]{0:T(1024)}, u32[]{:S(2)}) copy-start(f32[768]{0:T(1024)} %get-tuple-element.986) | copy-start | bytes 9220
  1491.3 47.9 %copy-start.39 = (f32[768]{0:T(1024)S(1)}, f32[768]{0:T(1024)}, u32[]{:S(2)}) copy-start(f32[768]{0:T(1024)} %get-tuple-element.987) | copy-start | bytes 9220
  1491.3 47.9 %copy-start.40 = (f32[768]{0:T(1024)S(1)}, f32[768]{0:T(1024)}, u32[]{:S(2)}) copy-start(f32[768]{0:T(1024)} %get-tuple-element.988) | copy-start | bytes 9220
  1491.4 47.9 %copy-start.41 = (f32[768]{0:T(1024)S(1)}, f32[768]{0:T(1024)}, u32[]{:S(2)}) copy-start(f32[768]{0:T(1024)} %get-tuple-element.989) | copy-start | bytes 9220
  (22 other events, 97.2 us)
Sparse Core Ops, SparseCore 0:
  53.4 88.2 all-gather.20
  145.0 71.2 all-gather.12
  219.6 71.3 all-gather.22
  294.1 71.3 all-gather.14
  367.4 279.9 all-gather.24
  649.4 279.1 all-gather.16
  930.7 279.1 all-gather.26
  1212.0 279.1 all-gather.18
where the time goes:
time: 1560 us
  waiting for transfers between devices  1250 us (80%)
  other arithmetic  173 us (11%)
  local copies, waits for them, and re-layouts  94.1 us (6%)
    all_gather x8, waiting for transfers between devices, prefix(): everything = jax.tree.map(lambda part: lax.all_gather(part, axis), shard)  1250 us
    select_n x96, other arithmetic, lap(): return jax.tree.map(lambda a, b: jnp.where(reached, a, b), new, before)  132 us
  transfers between devices with their start and end apart: 12, of which 9 were waited for; matrix products, arithmetic and copies ran while one was open for 12% of the time, Pallas kernels for 0%

commit v1 on v0

v1 whole, which is shorter than its diff:
```python
import functools

import jax
import jax.numpy as jnp
from jax import lax
from jax.experimental import pallas as pl
from jax.experimental.pallas import tpu as pltpu
from jax.sharding import PartitionSpec as P

MESH = pl.DeviceIdType.MESH
F32 = jnp.float32
BF16 = jnp.bfloat16
LOG2E = 1.4426950408889634
ROWS, COLS = 8, 16
LINE = 128
LANES = 128


def rounded(value):
    return value.astype(BF16).astype(F32)


def unit_norm(values):
    mean = jnp.mean(values, axis=-1, keepdims=True)
    centred = values - mean
    spread = jnp.mean(centred * centred, axis=-1, keepdims=True)
    return centred * lax.rsqrt(spread + 1e-05)


def softplus(value):
    return jnp.maximum(value, 0.0) + jnp.log1p(jnp.exp(-jnp.abs(value)))


def silu(value):
    return value / (1.0 + jnp.exp(-value))


def kernel(
    tokens, norm_gain, norm_bias, w_in, taps, conv_bias, w_xt, w_dt, dt_bias, a_log, d_skip, out_gain, out_bias, w_out,
    out,
    edge, edge_row, edge_col, halo, padded, conved, summed, gate, row_out, col_out, row_in, col_in,
    steps, drive, in_map, out_map, row_sum, col_sum, state_out, state_in,
    row_back_out, col_back_out, row_back_in, col_back_in,
    edge_send, edge_recv, row_send, row_recv, col_send, col_recv, state_send, state_recv,
    row_back_send, row_back_recv, col_back_send, col_back_recv,
):
    ny, nx = lax.axis_size("gy"), lax.axis_size("gx")
    my_y, my_x = lax.axis_index("gy"), lax.axis_index("gx")
    half_x, member_x = my_x // ROWS, lax.rem(my_x, ROWS)
    half_y, member_y = my_y // COLS, lax.rem(my_y, COLS)
    north, south = lax.rem(my_y + ny - 1, ny), lax.rem(my_y + 1, ny)
    west, east = lax.rem(my_x + nx - 1, nx), lax.rem(my_x + 1, nx)
    over_x = (my_y, lax.rem(my_x + ROWS, nx))
    over_y = (lax.rem(my_y + COLS, ny), my_x)
    around = [(north, my_x), (south, my_x), (my_y, west), (my_y, east), (north, west), (north, east), (south, west), (south, east)]

    def in_row(member):
        return (my_y, half_x * ROWS + member)

    def in_col(member):
        return (half_y * COLS + member, my_x)

    barrier = pltpu.get_barrier_semaphore()

    def greet(device):
        pl.semaphore_signal(barrier, inc=1, device_id=device, device_id_type=MESH)

    for device in around + [over_x, over_y]:
        greet(device)

    def greet_row(turn, carry):
        greet(in_row(lax.rem(member_x + turn, ROWS)))
        return carry

    def greet_col(turn, carry):
        greet(in_col(lax.rem(member_y + turn, COLS)))
        return carry

    lax.fori_loop(1, ROWS, greet_row, 0)
    lax.fori_loop(1, COLS, greet_col, 0)

    def copy(src, dst, send, recv, device):
        return pltpu.make_async_remote_copy(
            src_ref=src, dst_ref=dst, send_sem=send, recv_sem=recv, device_id=device, device_id_type=MESH
        )

    token_float = tokens[...].astype(F32)
    for r in range(ROWS):
        edge_col[0, r : r + 1, :] = token_float[r, 0:1, :]
        edge_col[1, r : r + 1, :] = token_float[r, COLS - 1 : COLS, :]
    edge_row[0] = tokens[0]
    edge_row[1] = tokens[ROWS - 1]
    pl.semaphore_wait(barrier, 10 + ROWS - 1 + COLS - 1)
    sends = [
        (edge_row.at[0], halo.at[1], 1, around[0]),
        (edge_row.at[1], halo.at[0], 0, around[1]),
        (edge_col.at[0], edge.at[1], 3, around[2]),
        (edge_col.at[1], edge.at[0], 2, around[3]),
        (edge_col.at[0], edge.at[5], 7, around[4]),
        (edge_col.at[1], edge.at[4], 6, around[5]),
        (edge_col.at[0], edge.at[3], 5, around[6]),
        (edge_col.at[1], edge.at[2], 4, around[7]),
    ]
    edges = [copy(src, dst, edge_send.at[slot], edge_recv.at[slot], device) for src, dst, slot, device in sends]
    for item in edges:
        item.start()

    gain, bias = norm_gain[...], norm_bias[...]

    def project(cells, weight):
        normed = (unit_norm(cells) * gain + bias).astype(BF16)
        return rounded(jnp.dot(normed, weight, preferred_element_type=F32))

    cells = token_float.reshape(ROWS * COLS, -1)
    normed = (unit_norm(cells) * gain + bias).astype(BF16)
    width = gate.shape[1]
    hw, groups = width // 2, width // LANES
    inner = rounded(jnp.dot(normed, w_in[:, :width], preferred_element_type=F32))
    padded[1 : 1 + ROWS, 8 : 8 + COLS, :] = inner.reshape(ROWS, COLS, width)
    gate[...] = rounded(jnp.dot(normed, w_in[:, width:], preferred_element_type=F32))

    for item in edges:
        item.wait_recv()
    rim = jnp.concatenate(
        [
            halo[0].astype(F32), halo[1].astype(F32), edge[0], edge[1],
            edge[2, 7:8, :], edge[3, 7:8, :], edge[4, 0:1, :], edge[5, 0:1, :], edge[2, 0:4, :],
        ],
        axis=0,
    )
    rim = project(rim, w_in[:, :width])
    has_n = (my_y > 0).astype(F32)
    has_s = (my_y < ny - 1).astype(F32)
    has_w = (my_x > 0).astype(F32)
    has_e = (my_x < nx - 1).astype(F32)
    padded[0, 8 : 8 + COLS, :] = rim[0:16] * has_n
    padded[1 + ROWS, 8 : 8 + COLS, :] = rim[16:32] * has_s
    for r in range(ROWS):
        padded[1 + r, 7:8, :] = rim[32 + r : 33 + r] * has_w
        padded[1 + r, 8 + COLS : 9 + COLS, :] = rim[40 + r : 41 + r] * has_e
    padded[0, 7:8, :] = rim[48:49] * (has_n * has_w)
    padded[0, 8 + COLS : 9 + COLS, :] = rim[49:50] * (has_n * has_e)
    padded[1 + ROWS, 7:8, :] = rim[50:51] * (has_s * has_w)
    padded[1 + ROWS, 8 + COLS : 9 + COLS, :] = rim[51:52] * (has_s * has_e)

    def row_copy(member):
        return copy(row_out.at[member], row_in.at[member_x], row_send.at[member], row_recv.at[member_x], in_row(member))

    def col_copy(member):
        return copy(col_out.at[member], col_in.at[member_y], col_send.at[member], col_recv.at[member_y], in_col(member))

    def conv_row(r, carry):
        total = jnp.broadcast_to(conv_bias[...], (COLS, width))
        for i in range(3):
            for j in range(3):
                tap = 3 * i + j
                total = total + padded[r + i, 7 + j : 7 + j + COLS, :] * taps[tap : tap + 1, :]
        value = silu(total).astype(BF16)
        row_out[r] = value
        for g in range(groups):
            conved[g, pl.ds(pl.multiple_of(r * COLS, COLS), COLS), :] = value[:, g * LANES : (g + 1) * LANES].astype(F32)

        @pl.when(r != member_x)
        def _():
            row_copy(r).start()

        return carry

    lax.fori_loop(0, ROWS, conv_row, 0)
    row_in[member_x] = row_out[member_x]
    for c in range(COLS):
        column = [conved[g, pl.ds(c, ROWS, stride=COLS), :] for g in range(groups)]
        for g in range(groups // 2):
            both = jnp.concatenate([column[g], column[g + groups // 2]], axis=0)
            col_out[c, :, g * LANES : (g + 1) * LANES] = both.astype(BF16)
    col_in[member_y] = col_out[member_y]

    def start_col(turn, carry):
        col_copy(lax.rem(member_y + turn, COLS)).start()
        return carry

    lax.fori_loop(1, COLS, start_col, 0)

    def split_columns(stacked):
        value = stacked.astype(F32)
        left, right = value[:, :ROWS, :], value[:, ROWS:, :]
        return jnp.concatenate([left.reshape(LINE, hw), right.reshape(LINE, hw)], axis=1)

    def prepare(cells, k):
        weight = w_xt[k]
        low = lax.dot_general(cells, weight, (((1,), (1,)), ((), ())), preferred_element_type=F32)
        maps = lax.dot_general(weight, cells, (((1,), (1,)), ((), ())), preferred_element_type=F32)
        low = low[:, :24].astype(BF16)
        step = softplus(jnp.dot(low, w_dt[k], preferred_element_type=F32) + dt_bias[pl.ds(k, 1), :])
        push = step * cells.astype(F32)
        for g in range(groups):
            steps[g, :LINE] = step[:, g * LANES : (g + 1) * LANES]
            drive[g, :LINE] = push[:, g * LANES : (g + 1) * LANES]
        ins, outs = maps[24:32], maps[32:40]

        def spread(block, carry):
            shift = lax.rem(LINE - 8 * block, LINE)
            ins_here, outs_here = pltpu.roll(ins, shift, 1), pltpu.roll(outs, shift, 1)
            for i in range(8):
                in_map[8 * block + i] = jnp.broadcast_to(ins_here[:, i : i + 1], (8, LANES))
                out_map[8 * block + i] = jnp.broadcast_to(outs_here[:, i : i + 1], (8, LANES))
            return carry

        lax.fori_loop(0, LINE // 8, spread, 0)

    sub = lax.broadcasted_iota(jnp.int32, (8, LANES), 0)

    def scan(k, backward, start, total, first):
        rates = -jnp.exp(a_log[k]) * LOG2E
        masks = [lax.rem(sub // s, 2) == backward for s in (1, 2, 4)]

        def chunk(turn, state):
            base = pl.multiple_of((turn + backward * (LINE // 8 - 1 - 2 * turn)) * 8, 8)
            cell = [base + i + backward * (7 - 2 * i) for i in range(8)]
            state = list(state)
            for g in range(width // LANES):
                lanes = slice(g * LANES, (g + 1) * LANES)
                parts = []
                for i in range(8):
                    step = steps[g, pl.ds(cell[i], 8, stride=0), :]
                    push = drive[g, pl.ds(cell[i], 8, stride=0), :]
                    state[g] = jnp.exp2(step * rates[:, lanes]) * state[g] + in_map[cell[i]] * push
                    parts.append(out_map[cell[i]] * state[g])
                for s, mask in zip((1, 2, 4), masks):
                    parts = [
                        jnp.where(mask, a, b) + pltpu.roll(jnp.where(mask, b, a), s, 0)
                        for a, b in zip(parts[0::2], parts[1::2])
                    ]
                here = (pl.ds(base, 8), lanes)
                total[here] = parts[0] if first else total[here] + parts[0]
            return tuple(state)

        return lax.fori_loop(0, LINE // 8, chunk, start)

    def split(state):
        return tuple(state[:, g * LANES : (g + 1) * LANES] for g in range(width // LANES))

    zero = tuple(jnp.zeros((8, LANES), F32) for _ in range(width // LANES))
    state_copies = [
        copy(state_out.at[0], state_in.at[0], state_send.at[0], state_recv.at[0], over_x),
        copy(state_out.at[1], state_in.at[1], state_send.at[1], state_recv.at[1], over_y),
    ]

    def wait_row(turn, carry):
        member = lax.rem(member_x + turn, ROWS)
        copy(row_out.at[member], row_in.at[member], row_send.at[member], row_recv.at[member], in_row(member)).wait_recv()
        return carry

    def wait_col(turn, carry):
        member = lax.rem(member_y + turn, COLS)
        copy(col_out.at[member], col_in.at[member], col_send.at[member], col_recv.at[member], in_col(member)).wait_recv()
        return carry

    def send_state(index, state):
        for g in range(width // LANES):
            state_out[index, :, g * LANES : (g + 1) * LANES] = state[g]
        state_copies[index].start()

    lax.fori_loop(1, ROWS, wait_row, 0)
    row_cells = row_in[...].reshape(LINE, width)
    prepare(row_cells, half_x)
    send_state(0, scan(half_x, half_x, zero, row_sum, True))

    lax.fori_loop(1, COLS, wait_col, 0)
    col_cells = split_columns(col_in[...]).astype(BF16)
    prepare(col_cells, 2 + half_y)
    send_state(1, scan(2 + half_y, half_y, zero, col_sum, True))

    prepare(row_cells, 1 - half_x)
    state_copies[0].wait_recv()
    scan(1 - half_x, 1 - half_x, split(state_in[0]), row_sum, False)
    row_back_out[...] = row_sum[...].astype(BF16).reshape(ROWS, COLS, width)
    row_back_in[member_x] = row_back_out[member_x]

    def row_back(member, slot):
        return copy(row_back_out.at[member], row_back_in.at[slot], row_back_send.at[member], row_back_recv.at[slot], in_row(member))

    def col_back(member, slot):
        return copy(col_back_out.at[member], col_back_in.at[slot], col_back_send.at[member], col_back_recv.at[slot], in_col(member))

    def start_row_back(turn, carry):
        row_back(lax.rem(member_x + turn, ROWS), member_x).start()
        return carry

    lax.fori_loop(1, ROWS, start_row_back, 0)

    prepare(col_cells, 3 - half_y)
    state_copies[1].wait_recv()
    scan(3 - half_y, 1 - half_y, split(state_in[1]), col_sum, False)
    col_value = col_sum[...].reshape(COLS, ROWS, width)
    col_back_out[...] = jnp.concatenate([col_value[:, :, :hw], col_value[:, :, hw:]], axis=1).astype(BF16)
    col_back_in[member_y] = col_back_out[member_y]

    def start_col_back(turn, carry):
        col_back(lax.rem(member_y + turn, COLS), member_y).start()
        return carry

    lax.fori_loop(1, COLS, start_col_back, 0)

    def wait_row_back(turn, carry):
        member = lax.rem(member_x + turn, ROWS)
        row_back(member, member).wait_recv()
        return carry

    def wait_col_back(turn, carry):
        member = lax.rem(member_y + turn, COLS)
        col_back(member, member).wait_recv()
        return carry

    lax.fori_loop(1, ROWS, wait_row_back, 0)
    skip = jnp.sum(d_skip[...], axis=0, keepdims=True)
    row_value = row_back_in[...].reshape(LINE, width).astype(F32)
    for g in range(groups):
        lanes = slice(g * LANES, (g + 1) * LANES)
        summed[g, :LINE] = row_value[:, lanes] + skip[:, lanes] * conved[g, :LINE]
    lax.fori_loop(1, COLS, wait_col_back, 0)
    for c in range(COLS):
        value = col_back_in[c].astype(F32)
        for g in range(groups):
            here = (g, pl.ds(c, ROWS, stride=COLS), slice(None))
            low, high = (0, ROWS) if g < groups // 2 else (ROWS, 2 * ROWS)
            lane = (g % (groups // 2)) * LANES
            summed[here] = summed[here] + value[low:high, lane : lane + LANES]
    total = jnp.concatenate([summed[g, :LINE] for g in range(groups)], axis=1)
    gated = (unit_norm(total) * out_gain[...] + out_bias[...]) * silu(gate[...])
    mixed = tokens[...].astype(F32).reshape(ROWS * COLS, -1) + jnp.dot(gated.astype(BF16), w_out[...], preferred_element_type=F32)
    out[...] = mixed.reshape(out.shape).astype(BF16)

    for item in edges + state_copies:
        item.wait_send()

    def drain_row(turn, carry):
        member = lax.rem(member_x + turn, ROWS)
        row_copy(member).wait_send()
        row_back(member, member_x).wait_send()
        return carry

    def drain_col(turn, carry):
        member = lax.rem(member_y + turn, COLS)
        col_copy(member).wait_send()
        col_back(member, member_y).wait_send()
        return carry

    lax.fori_loop(1, ROWS, drain_row, 0)
    lax.fori_loop(1, COLS, drain_col, 0)


def shards(tokens, norm_gain, norm_bias, w_in, conv_taps, conv_bias, w_x, w_dt, dt_bias, a_log, d_skip, out_gain, out_bias, w_out):
    chans, width = tokens.shape[-1], w_out.shape[0]
    hw = width // 2
    dma = pltpu.SemaphoreType.DMA
    vmem = pl.BlockSpec(memory_space=pltpu.VMEM)
    return pl.pallas_call(
        kernel,
        out_shape=jax.ShapeDtypeStruct(tokens.shape, tokens.dtype),
        in_specs=[vmem] * 14,
        out_specs=vmem,
        scratch_shapes=[
            pltpu.VMEM((6, ROWS, chans), F32),
            pltpu.VMEM((2, COLS, chans), BF16),
            pltpu.VMEM((2, ROWS, chans), F32),
            pltpu.VMEM((2, COLS, chans), BF16),
            pltpu.VMEM((ROWS + 2, COLS + 16, width), F32),
            pltpu.VMEM((width // LANES, LINE + COLS, LANES), F32),
            pltpu.VMEM((width // LANES, LINE + COLS, LANES), F32),
            pltpu.VMEM((ROWS * COLS, width), F32),
            pltpu.VMEM((ROWS, COLS, width), BF16),
            pltpu.VMEM((COLS, 2 * ROWS, hw), BF16),
            pltpu.VMEM((ROWS, COLS, width), BF16),
            pltpu.VMEM((COLS, 2 * ROWS, hw), BF16),
            pltpu.VMEM((width // LANES, LINE + 8, LANES), F32),
            pltpu.VMEM((width // LANES, LINE + 8, LANES), F32),
            pltpu.VMEM((LINE, 8, LANES), F32),
            pltpu.VMEM((LINE, 8, LANES), F32),
            pltpu.VMEM((LINE, width), F32),
            pltpu.VMEM((LINE, width), F32),
            pltpu.VMEM((2, 8, width), F32),
            pltpu.VMEM((2, 8, width), F32),
            pltpu.VMEM((ROWS, COLS, width), BF16),
            pltpu.VMEM((COLS, 2 * ROWS, hw), BF16),
            pltpu.VMEM((ROWS, COLS, width), BF16),
            pltpu.VMEM((COLS, 2 * ROWS, hw), BF16),
            dma((8,)), dma((8,)), dma((ROWS,)), dma((ROWS,)), dma((COLS,)), dma((COLS,)), dma((2,)), dma((2,)),
            dma((ROWS,)), dma((ROWS,)), dma((COLS,)), dma((COLS,)),
        ],
        compiler_params=pltpu.CompilerParams(collective_id=0, has_side_effects=True, vmem_limit_bytes=40 * 1024 * 1024),
    )(
        tokens, norm_gain.reshape(1, -1), norm_bias.reshape(1, -1), w_in, conv_taps, conv_bias.reshape(1, -1),
        jnp.transpose(w_x, (0, 2, 1)), w_dt, dt_bias, a_log, d_skip, out_gain.reshape(1, -1), out_bias.reshape(1, -1), w_out,
    )


def solution(mesh):
    placed = (P("gy", "gx", None),) + (P(),) * 13
    return jax.shard_map(shards, mesh=mesh, in_specs=placed, out_specs=P("gy", "gx", None), check_vma=False)
```

time: 1560 us -> 63.1 us (0.04)
  waiting for transfers between devices: 1250 us -> 0 us
  other arithmetic: 173 us -> 0 us
  local copies, waits for them, and re-layouts: 94.1 us -> 12.3 us
  Pallas kernels: 0 us -> 50.2 us
    all_gather x8 -> x0, waiting for transfers between devices: 1250 us -> none  [prefix(): everything = jax.tree.map(lambda part: lax.all_gather(part, axis), shard)]
    select_n x96 -> x0, other arithmetic: 132 us -> none  [lap(): return jax.tree.map(lambda a, b: jnp.where(reached, a, b), new, before)]
    pallas_call x0 -> x1, Pallas kernels: none -> 50.2 us  [shards(): pl.pallas_call(kernel, out_shape=jax.ShapeDtypeStruct(tokens.shape, token...]
    mul x80 -> x0, local copies, waits for them, and re-layouts: 37.8 us -> none  [the longest x38 19.2 us: shards(): out_maps[..., state_index][..., None]]
    dynamic_update_slice x64 -> x0, local copies, waits for them, and re-layouts: 28.5 us -> none  [local_scan(): final, outputs = lax.scan(advance, start, (drive, steps, in_maps, out_maps))]
    reduce_sum x52 -> x0, other arithmetic: 23.6 us -> none  [the longest x48 17.4 us: advance(): return (state, jnp.sum(out_map.T[:, :, None] * state, axis=0))]
  transfers between devices with their start and end apart: 12 -> 0, of which waited for: 9 -> 0; matrix products, arithmetic and copies ran while one was open for 12% -> 0% of each run, Pallas kernels for 0% -> 0%
where the time goes in v1:
time: 63.1 us; the launch traced here: 62.4 us
  Pallas kernels  50.2 us (80%)
  local copies, waits for them, and re-layouts  12.3 us (19%)
    pallas_call x1, Pallas kernels, shards(): pl.pallas_call(kernel, out_shape=jax.ShapeDtypeStruct(tokens.shape, token...  50.2 us
    unnamed x19, local copies, waits for them, and re-layouts  8.82 us

profile of v1, /device:TPU:1, one launch (start us, length us, event | category | flops | bytes accessed | tf_op | source)
XLA Modules:
  0.0 62.4 jit_solution(9736840647383194753)
XLA Ops:
  0.0 0.7 %reshape.15.norm_gain = f32[1,384]{1,0:T(1,128)S(1)} reshape(f32[384]{0:T(512)} %param.15) | data formatting | bytes 3072 | tf_op jit(solution)/shard_map/reshape | solution.py:393
  0.7 0.7 %reshape.16.norm_bias = f32[1,384]{1,0:T(1,128)S(1)} reshape(f32[384]{0:T(512)} %param.16) | data formatting | bytes 3072 | tf_op jit(solution)/shard_map/reshape | solution.py:393
  1.4 0.7 %reshape.17.conv_bias = f32[1,768]{1,0:T(1,128)S(1)} reshape(f32[768]{0:T(1024)} %param.19) | data formatting | bytes 6144 | tf_op jit(solution)/shard_map/reshape | solution.py:393
  2.1 0.7 %reshape.18.out_gain = f32[1,768]{1,0:T(1,128)S(1)} reshape(f32[768]{0:T(1024)} %param.25) | data formatting | bytes 6144 | tf_op jit(solution)/shard_map/reshape | solution.py:394
  2.7 0.7 %reshape.19.out_bias = f32[1,768]{1,0:T(1,128)S(1)} reshape(f32[768]{0:T(1024)} %param.26) | data formatting | bytes 6144 | tf_op jit(solution)/shard_map/reshape | solution.py:394
  3.4 0.0 copy-start
  3.4 1.3 %copy-done = bf16[384,1536]{1,0:T(8,128)(2,1)S(1)} copy-done((bf16[384,1536]{1,0:T(8,128)(2,1)S(1)}, bf16[384,1536]{1,0:T(8,128)(2,1)}, u32[]{:S(2)}) %copy-start) | copy-done | bytes 1179672
  4.7 0.0 copy-start.1
  4.7 1.1 %copy-done.1 = bf16[768,384]{1,0:T(8,128)(2,1)S(1)} copy-done((bf16[768,384]{1,0:T(8,128)(2,1)S(1)}, bf16[768,384]{1,0:T(8,128)(2,1)}, u32[]{:S(2)}) %copy-start.1) | copy-done | bytes 589848
  5.8 0.0 copy-start.2
  5.8 0.9 %copy-done.2 = bf16[4,768,40]{1,2,0:T(8,128)(2,1)S(1)} copy-done((bf16[4,768,40]{1,2,0:T(8,128)(2,1)S(1)}, bf16[4,768,40]{1,2,0:T(8,128)(2,1)}, u32[]{:S(2)}) %copy-start.2) | copy-done | bytes 245784
  6.7 0.0 copy-start.3
  6.7 0.9 %copy-done.3 = bf16[4,24,768]{2,1,0:T(8,128)(2,1)S(1)} copy-done((bf16[4,24,768]{2,1,0:T(8,128)(2,1)S(1)}, bf16[4,24,768]{2,1,0:T(8,128)(2,1)}, u32[]{:S(2)}) %copy-start.3) | copy-done | bytes 147480
  7.6 0.0 copy-start.4
  7.6 0.9 %copy-done.4 = bf16[8,16,384]{2,1,0:T(8,128)(2,1)S(1)} copy-done((bf16[8,16,384]{2,1,0:T(8,128)(2,1)S(1)}, bf16[8,16,384]{2,1,0:T(8,128)(2,1)}, u32[]{:S(2)}) %copy-start.4) | copy-done | bytes 98328
  8.5 0.0 copy-start.5
  8.5 0.9 %copy-done.5 = f32[4,8,768]{2,1,0:T(8,128)S(1)} copy-done((f32[4,8,768]{2,1,0:T(8,128)S(1)}, f32[4,8,768]{2,1,0:T(8,128)}, u32[]{:S(2)}) %copy-start.5) | copy-done | bytes 98328
  9.4 0.0 copy-start.6
  9.4 0.8 %copy-done.6 = f32[9,768]{1,0:T(8,128)S(1)} copy-done((f32[9,768]{1,0:T(8,128)S(1)}, f32[9,768]{1,0:T(8,128)}, u32[]{:S(2)}) %copy-start.6) | copy-done | bytes 27672
  10.2 0.0 copy-start.7
  10.2 0.7 %copy-done.7 = f32[4,768]{1,0:T(4,128)S(1)} copy-done((f32[4,768]{1,0:T(4,128)S(1)}, f32[4,768]{1,0:T(4,128)}, u32[]{:S(2)}) %copy-start.7) | copy-done | bytes 12312
  10.9 0.0 copy-start.8
  10.9 0.7 %copy-done.8 = f32[4,768]{1,0:T(4,128)S(1)} copy-done((f32[4,768]{1,0:T(4,128)S(1)}, f32[4,768]{1,0:T(4,128)}, u32[]{:S(2)}) %copy-start.8) | copy-done | bytes 12312
  11.6 50.2 %shard_map.136 = bf16[8,16,384]{2,1,0:T(8,128)(2,1)S(1)} custom-call(bf16[8,16,384]{2,1,0:T(8,128)(2,1)S(1)} %copy-done.4, f32[1,384]{1,0:T(1,128)S(1)} %reshape.15.norm_gain, f32[1,384]{1,0:T(1,128)S(1)} %reshape.16.norm_bias, bf16[384,1536]{1,0:T(8,128)(2,1)S(1)} %copy-done, f32[9,768]{1,0:T(8,128)S(1)} %copy-done.6, f32[1,768]{1,0:T(1,128)S(1)} %reshape.17.conv_bias, ...), custom_call_target="tpu_custom_call" | custom-call | tf_op jit(solution)/shard_map/pallas_call | solution.py:358
  61.8 0.6 %copy.16 = bf16[8,16,384]{2,1,0:T(8,128)(2,1)} copy(bf16[8,16,384]{2,1,0:T(8,128)(2,1)S(1)} %shard_map.136) | data formatting | bytes 196608
Async XLA Ops:
  3.4 1.3 %copy-start = (bf16[384,1536]{1,0:T(8,128)(2,1)S(1)}, bf16[384,1536]{1,0:T(8,128)(2,1)}, u32[]{:S(2)}) copy-start(bf16[384,1536]{1,0:T(8,128)(2,1)} %w_in.1) | copy-start | bytes 3538948
  4.7 1.1 %copy-start.1 = (bf16[768,384]{1,0:T(8,128)(2,1)S(1)}, bf16[768,384]{1,0:T(8,128)(2,1)}, u32[]{:S(2)}) copy-start(bf16[768,384]{1,0:T(8,128)(2,1)} %w_out.1) | copy-start | bytes 1769476
  5.8 0.9 %copy-start.2 = (bf16[4,768,40]{1,2,0:T(8,128)(2,1)S(1)}, bf16[4,768,40]{1,2,0:T(8,128)(2,1)}, u32[]{:S(2)}) copy-start(bf16[4,768,40]{1,2,0:T(8,128)(2,1)} %param.20) | copy-start | bytes 737284
  6.7 0.9 %copy-start.3 = (bf16[4,24,768]{2,1,0:T(8,128)(2,1)S(1)}, bf16[4,24,768]{2,1,0:T(8,128)(2,1)}, u32[]{:S(2)}) copy-start(bf16[4,24,768]{2,1,0:T(8,128)(2,1)} %w_dt.1) | copy-start | bytes 442372
  7.6 0.9 %copy-start.4 = (bf16[8,16,384]{2,1,0:T(8,128)(2,1)S(1)}, bf16[8,16,384]{2,1,0:T(8,128)(2,1)}, u32[]{:S(2)}) copy-start(bf16[8,16,384]{2,1,0:T(8,128)(2,1)} %tokens.1) | copy-start | bytes 294916
  8.5 0.9 %copy-start.5 = (f32[4,8,768]{2,1,0:T(8,128)S(1)}, f32[4,8,768]{2,1,0:T(8,128)}, u32[]{:S(2)}) copy-start(f32[4,8,768]{2,1,0:T(8,128)} %a_log.1) | copy-start | bytes 294916
  9.4 0.8 %copy-start.6 = (f32[9,768]{1,0:T(8,128)S(1)}, f32[9,768]{1,0:T(8,128)}, u32[]{:S(2)}) copy-start(f32[9,768]{1,0:T(8,128)} %taps.1) | copy-start | bytes 82948
  10.2 0.7 %copy-start.7 = (f32[4,768]{1,0:T(4,128)S(1)}, f32[4,768]{1,0:T(4,128)}, u32[]{:S(2)}) copy-start(f32[4,768]{1,0:T(4,128)} %dt_bias.1) | copy-start | bytes 36868
  10.9 0.7 %copy-start.8 = (f32[4,768]{1,0:T(4,128)S(1)}, f32[4,768]{1,0:T(4,128)}, u32[]{:S(2)}) copy-start(f32[4,768]{1,0:T(4,128)} %d_skip.1) | copy-start | bytes 36868

commit v2 on v1

--- a/solution.py
+++ b/solution.py
@@ -36,10 +36,13 @@
 
 
 def kernel(
-    tokens, norm_gain, norm_bias, w_in, taps, conv_bias, w_xt, w_dt, dt_bias, a_log, d_skip, out_gain, out_bias, w_out,
+    tokens_hbm, w_in_hbm, norm_gain_hbm, norm_bias_hbm, taps_hbm, conv_bias_hbm, w_xt_hbm, w_dt_hbm, dt_bias_hbm, a_log_hbm,
+    d_skip_hbm, out_gain_hbm, out_bias_hbm, w_out_hbm,
     out,
+    tokens, w_in, norm_gain, norm_bias, taps, conv_bias, w_xt, w_dt, dt_bias, a_log, d_skip, out_gain, out_bias, w_out,
+    load_sem,
     edge, edge_row, edge_col, halo, padded, conved, summed, gate, row_out, col_out, row_in, col_in,
-    steps, drive, in_map, out_map, row_sum, col_sum, state_out, state_in,
+    cell_maps, steps, drive, in_map, out_map, row_sum, col_sum, state_out, state_in,
     row_back_out, col_back_out, row_back_in, col_back_in,
     edge_send, edge_recv, row_send, row_recv, col_send, col_recv, state_send, state_recv,
     row_back_send, row_back_recv, col_back_send, col_back_recv,
@@ -47,18 +50,29 @@
     ny, nx = lax.axis_size("gy"), lax.axis_size("gx")
     my_y, my_x = lax.axis_index("gy"), lax.axis_index("gx")
     half_x, member_x = my_x // ROWS, lax.rem(my_x, ROWS)
-    half_y, member_y = my_y // COLS, lax.rem(my_y, COLS)
+    member_y = lax.rem(my_y, COLS)
+    half_y = lax.rem(my_x, 2)
+    own_col = (my_y // COLS == half_y).astype(jnp.int32)
     north, south = lax.rem(my_y + ny - 1, ny), lax.rem(my_y + 1, ny)
     west, east = lax.rem(my_x + nx - 1, nx), lax.rem(my_x + 1, nx)
     over_x = (my_y, lax.rem(my_x + ROWS, nx))
-    over_y = (lax.rem(my_y + COLS, ny), my_x)
+    over_y = (my_y, my_x + 1 - 2 * half_y)
     around = [(north, my_x), (south, my_x), (my_y, west), (my_y, east), (north, west), (north, east), (south, west), (south, east)]
 
     def in_row(member):
         return (my_y, half_x * ROWS + member)
 
     def in_col(member):
-        return (half_y * COLS + member, my_x)
+        return (half_y * COLS + member, my_x - half_y + my_y // COLS)
+
+    pairs = [
+        (tokens_hbm, tokens), (w_in_hbm, w_in), (norm_gain_hbm, norm_gain), (norm_bias_hbm, norm_bias), (taps_hbm, taps),
+        (conv_bias_hbm, conv_bias), (w_xt_hbm, w_xt), (w_dt_hbm, w_dt), (dt_bias_hbm, dt_bias), (a_log_hbm, a_log),
+        (d_skip_hbm, d_skip), (out_gain_hbm, out_gain), (out_bias_hbm, out_bias), (w_out_hbm, w_out),
+    ]
+    loads = [pltpu.make_async_copy(src, dst, load_sem.at[i]) for i, (src, dst) in enumerate(pairs)]
+    for item in loads:
+        item.start()
 
     barrier = pltpu.get_barrier_semaphore()
 
@@ -77,20 +91,21 @@
         return carry
 
     lax.fori_loop(1, ROWS, greet_row, 0)
-    lax.fori_loop(1, COLS, greet_col, 0)
+    lax.fori_loop(own_col, COLS, greet_col, 0)
 
     def copy(src, dst, send, recv, device):
         return pltpu.make_async_remote_copy(
             src_ref=src, dst_ref=dst, send_sem=send, recv_sem=recv, device_id=device, device_id_type=MESH
         )
 
+    loads[0].wait()
     token_float = tokens[...].astype(F32)
     for r in range(ROWS):
         edge_col[0, r : r + 1, :] = token_float[r, 0:1, :]
         edge_col[1, r : r + 1, :] = token_float[r, COLS - 1 : COLS, :]
     edge_row[0] = tokens[0]
     edge_row[1] = tokens[ROWS - 1]
-    pl.semaphore_wait(barrier, 10 + ROWS - 1 + COLS - 1)
+    pl.semaphore_wait(barrier, 10 + ROWS - 1 + COLS - own_col)
     sends = [
         (edge_row.at[0], halo.at[1], 1, around[0]),
         (edge_row.at[1], halo.at[0], 0, around[1]),
@@ -105,7 +120,9 @@
     for item in edges:
         item.start()
 
-    gain, bias = norm_gain[...], norm_bias[...]
+    for item in loads[1:]:
+        item.wait()
+    gain, bias = norm_gain[...].reshape(1, -1), norm_bias[...].reshape(1, -1)
 
     def project(cells, weight):
         normed = (unit_norm(cells) * gain + bias).astype(BF16)
@@ -150,7 +167,7 @@
         return copy(col_out.at[member], col_in.at[member_y], col_send.at[member], col_recv.at[member_y], in_col(member))
 
     def conv_row(r, carry):
-        total = jnp.broadcast_to(conv_bias[...], (COLS, width))
+        total = jnp.broadcast_to(conv_bias[...].reshape(1, -1), (COLS, width))
         for i in range(3):
             for j in range(3):
                 tap = 3 * i + j
@@ -173,40 +190,53 @@
         for g in range(groups // 2):
             both = jnp.concatenate([column[g], column[g + groups // 2]], axis=0)
             col_out[c, :, g * LANES : (g + 1) * LANES] = both.astype(BF16)
-    col_in[member_y] = col_out[member_y]
+
+    @pl.when(own_col == 1)
+    def _():
+        col_in[member_y] = col_out[member_y]
 
     def start_col(turn, carry):
         col_copy(lax.rem(member_y + turn, COLS)).start()
         return carry
 
-    lax.fori_loop(1, COLS, start_col, 0)
+    lax.fori_loop(own_col, COLS, start_col, 0)
 
     def split_columns(stacked):
         value = stacked.astype(F32)
         left, right = value[:, :ROWS, :], value[:, ROWS:, :]
         return jnp.concatenate([left.reshape(LINE, hw), right.reshape(LINE, hw)], axis=1)
 
-    def prepare(cells, k):
-        weight = w_xt[k]
-        low = lax.dot_general(cells, weight, (((1,), (1,)), ((), ())), preferred_element_type=F32)
-        maps = lax.dot_general(weight, cells, (((1,), (1,)), ((), ())), preferred_element_type=F32)
-        low = low[:, :24].astype(BF16)
-        step = softplus(jnp.dot(low, w_dt[k], preferred_element_type=F32) + dt_bias[pl.ds(k, 1), :])
-        push = step * cells.astype(F32)
-        for g in range(groups):
-            steps[g, :LINE] = step[:, g * LANES : (g + 1) * LANES]
-            drive[g, :LINE] = push[:, g * LANES : (g + 1) * LANES]
-        ins, outs = maps[24:32], maps[32:40]
-
-        def spread(block, carry):
-            shift = lax.rem(LINE - 8 * block, LINE)
-            ins_here, outs_here = pltpu.roll(ins, shift, 1), pltpu.roll(outs, shift, 1)
-            for i in range(8):
-                in_map[8 * block + i] = jnp.broadcast_to(ins_here[:, i : i + 1], (8, LANES))
-                out_map[8 * block + i] = jnp.broadcast_to(outs_here[:, i : i + 1], (8, LANES))
-            return carry
-
-        lax.fori_loop(0, LINE // 8, spread, 0)
+    eighth = lax.broadcasted_iota(jnp.int32, (LANES, 4 * LANES), 0) // 8
+    block = lax.broadcasted_iota(jnp.int32, (LANES, 4 * LANES), 1) // LANES
+    pick = ((eighth == block + jnp.where(block < 2, 3, 6)) | (eighth == block + 10)).astype(F32).astype(BF16)
+    lane = lax.broadcasted_iota(jnp.int32, (8, LANES), 1)
+    own_state = lane % 8 == lax.broadcasted_iota(jnp.int32, (8, LANES), 0)
+
+    def prepare(cells, first):
+        weight = w_xt[40 * first : 40 * first + 80, :]
+        proj = lax.dot_general(cells, weight, (((1,), (1,)), ((), ())), preferred_element_type=F32)
+        cells_float = cells.astype(F32)
+        ranks = w_dt[...].astype(F32)
+        for side in range(2):
+            k = first + side
+            low = proj[:, 40 * side : 40 * side + 24].astype(BF16)
+            rank = ranks[24 * k : 24 * k + 24].astype(BF16)
+            step = softplus(jnp.dot(low, rank, preferred_element_type=F32) + dt_bias[k : k + 1, :])
+            push = step * cells_float
+            for g in range(groups):
+                steps[k, g, :LINE] = step[:, g * LANES : (g + 1) * LANES]
+                drive[k, g, :LINE] = push[:, g * LANES : (g + 1) * LANES]
+        proj = jnp.concatenate([proj, jnp.zeros((LINE, LANES - 80), F32)], axis=1)
+        high = rounded(proj)
+        left = rounded(proj - high)
+        wide = lax.broadcasted_iota(jnp.int32, (LINE, LANES), 1)
+        cell_maps[:LINE] = jnp.where(wide < 80, high, jnp.where(wide < 96, pltpu.roll(left, 56, 1), pltpu.roll(left, 32, 1)))
+        rows = [jnp.where(own_state, cell_maps[pl.ds(cell, 8, stride=0), :], 0.0) for cell in range(LINE)]
+        maps = jnp.dot(jnp.concatenate(rows, axis=0).astype(BF16), pick, preferred_element_type=F32)
+        maps = maps.reshape(LINE, 8, 4 * LANES)
+        for side in range(2):
+            in_map[first + side] = maps[:, :, 2 * side * LANES : (2 * side + 1) * LANES]
+            out_map[first + side] = maps[:, :, (2 * side + 1) * LANES : (2 * side + 2) * LANES]
 
     sub = lax.broadcasted_iota(jnp.int32, (8, LANES), 0)
 
@@ -222,10 +252,10 @@
                 lanes = slice(g * LANES, (g + 1) * LANES)
                 parts = []
                 for i in range(8):
-                    step = steps[g, pl.ds(cell[i], 8, stride=0), :]
-                    push = drive[g, pl.ds(cell[i], 8, stride=0), :]
-                    state[g] = jnp.exp2(step * rates[:, lanes]) * state[g] + in_map[cell[i]] * push
-                    parts.append(out_map[cell[i]] * state[g])
+                    step = steps[k, g, pl.ds(cell[i], 8, stride=0), :]
+                    push = drive[k, g, pl.ds(cell[i], 8, stride=0), :]
+                    state[g] = jnp.exp2(step * rates[:, lanes]) * state[g] + in_map[k, cell[i]] * push
+                    parts.append(out_map[k, cell[i]] * state[g])
                 for s, mask in zip((1, 2, 4), masks):
                     parts = [
                         jnp.where(mask, a, b) + pltpu.roll(jnp.where(mask, b, a), s, 0)
@@ -263,15 +293,14 @@
 
     lax.fori_loop(1, ROWS, wait_row, 0)
     row_cells = row_in[...].reshape(LINE, width)
-    prepare(row_cells, half_x)
+    prepare(row_cells, 0)
     send_state(0, scan(half_x, half_x, zero, row_sum, True))
 
-    lax.fori_loop(1, COLS, wait_col, 0)
+    lax.fori_loop(own_col, COLS, wait_col, 0)
     col_cells = split_columns(col_in[...]).astype(BF16)
-    prepare(col_cells, 2 + half_y)
+    prepare(col_cells, 2)
     send_state(1, scan(2 + half_y, half_y, zero, col_sum, True))
 
-    prepare(row_cells, 1 - half_x)
     state_copies[0].wait_recv()
     scan(1 - half_x, 1 - half_x, split(state_in[0]), row_sum, False)
     row_back_out[...] = row_sum[...].astype(BF16).reshape(ROWS, COLS, width)
@@ -289,18 +318,20 @@
 
     lax.fori_loop(1, ROWS, start_row_back, 0)
 
-    prepare(col_cells, 3 - half_y)
     state_copies[1].wait_recv()
     scan(3 - half_y, 1 - half_y, split(state_in[1]), col_sum, False)
     col_value = col_sum[...].reshape(COLS, ROWS, width)
     col_back_out[...] = jnp.concatenate([col_value[:, :, :hw], col_value[:, :, hw:]], axis=1).astype(BF16)
-    col_back_in[member_y] = col_back_out[member_y]
+
+    @pl.when(own_col == 1)
+    def _():
+        col_back_in[member_y] = col_back_out[member_y]
 
     def start_col_back(turn, carry):
         col_back(lax.rem(member_y + turn, COLS), member_y).start()
         return carry
 
-    lax.fori_loop(1, COLS, start_col_back, 0)
+    lax.fori_loop(own_col, COLS, start_col_back, 0)
 
     def wait_row_back(turn, carry):
         member = lax.rem(member_x + turn, ROWS)
@@ -318,7 +349,7 @@
     for g in range(groups):
         lanes = slice(g * LANES, (g + 1) * LANES)
         summed[g, :LINE] = row_value[:, lanes] + skip[:, lanes] * conved[g, :LINE]
-    lax.fori_loop(1, COLS, wait_col_back, 0)
+    lax.fori_loop(own_col, COLS, wait_col_back, 0)
     for c in range(COLS):
         value = col_back_in[c].astype(F32)
         for g in range(groups):
@@ -327,7 +358,7 @@
             lane = (g % (groups // 2)) * LANES
             summed[here] = summed[here] + value[low:high, lane : lane + LANES]
     total = jnp.concatenate([summed[g, :LINE] for g in range(groups)], axis=1)
-    gated = (unit_norm(total) * out_gain[...] + out_bias[...]) * silu(gate[...])
+    gated = (unit_norm(total) * out_gain[...].reshape(1, -1) + out_bias[...].reshape(1, -1)) * silu(gate[...])
     mixed = tokens[...].astype(F32).reshape(ROWS * COLS, -1) + jnp.dot(gated.astype(BF16), w_out[...], preferred_element_type=F32)
     out[...] = mixed.reshape(out.shape).astype(BF16)
 
@@ -347,20 +378,24 @@
         return carry
 
     lax.fori_loop(1, ROWS, drain_row, 0)
-    lax.fori_loop(1, COLS, drain_col, 0)
+    lax.fori_loop(own_col, COLS, drain_col, 0)
 
 
 def shards(tokens, norm_gain, norm_bias, w_in, conv_taps, conv_bias, w_x, w_dt, dt_bias, a_log, d_skip, out_gain, out_bias, w_out):
     chans, width = tokens.shape[-1], w_out.shape[0]
     hw = width // 2
     dma = pltpu.SemaphoreType.DMA
-    vmem = pl.BlockSpec(memory_space=pltpu.VMEM)
+    operands = (
+        tokens, w_in, norm_gain, norm_bias, conv_taps, conv_bias, jnp.transpose(w_x, (0, 2, 1)).reshape(-1, width),
+        w_dt.reshape(-1, width), dt_bias, a_log, d_skip, out_gain, out_bias, w_out,
+    )
     return pl.pallas_call(
         kernel,
         out_shape=jax.ShapeDtypeStruct(tokens.shape, tokens.dtype),
-        in_specs=[vmem] * 14,
-        out_specs=vmem,
-        scratch_shapes=[
+        in_specs=[pl.BlockSpec(memory_space=pltpu.MemorySpace.HBM)] * 14,
+        out_specs=pl.BlockSpec(memory_space=pltpu.VMEM),
+        scratch_shapes=[pltpu.VMEM(value.shape, value.dtype) for value in operands] + [
+            dma((14,)),
             pltpu.VMEM((6, ROWS, chans), F32),
             pltpu.VMEM((2, COLS, chans), BF16),
             pltpu.VMEM((2, ROWS, chans), F32),
@@ -373,10 +408,11 @@
             pltpu.VMEM((COLS, 2 * ROWS, hw), BF16),
             pltpu.VMEM((ROWS, COLS, width), BF16),
             pltpu.VMEM((COLS, 2 * ROWS, hw), BF16),
-            pltpu.VMEM((width // LANES, LINE + 8, LANES), F32),
-            pltpu.VMEM((width // LANES, LINE + 8, LANES), F32),
-            pltpu.VMEM((LINE, 8, LANES), F32),
-            pltpu.VMEM((LINE, 8, LANES), F32),
+            pltpu.VMEM((LINE + 8, LANES), F32),
+            pltpu.VMEM((4, width // LANES, LINE + 8, LANES), F32),
+            pltpu.VMEM((4, width // LANES, LINE + 8, LANES), F32),
+            pltpu.VMEM((4, LINE, 8, LANES), F32),
+            pltpu.VMEM((4, LINE, 8, LANES), F32),
             pltpu.VMEM((LINE, width), F32),
             pltpu.VMEM((LINE, width), F32),
             pltpu.VMEM((2, 8, width), F32),
@@ -388,11 +424,8 @@
             dma((8,)), dma((8,)), dma((ROWS,)), dma((ROWS,)), dma((COLS,)), dma((COLS,)), dma((2,)), dma((2,)),
             dma((ROWS,)), dma((ROWS,)), dma((COLS,)), dma((COLS,)),
         ],
-        compiler_params=pltpu.CompilerParams(collective_id=0, has_side_effects=True, vmem_limit_bytes=40 * 1024 * 1024),
-    )(
-        tokens, norm_gain.reshape(1, -1), norm_bias.reshape(1, -1), w_in, conv_taps, conv_bias.reshape(1, -1),
-        jnp.transpose(w_x, (0, 2, 1)), w_dt, dt_bias, a_log, d_skip, out_gain.reshape(1, -1), out_bias.reshape(1, -1), w_out,
-    )
+        compiler_params=pltpu.CompilerParams(collective_id=0, has_side_effects=True, vmem_limit_bytes=60 * 1024 * 1024),
+    )(*operands)
 
 
 def solution(mesh):

time: 63.1 us -> 47.3 us (0.75)
  local copies, waits for them, and re-layouts: 12.3 us -> 1.54 us
  Pallas kernels: 50.2 us -> 45.6 us
    unnamed x19 -> x1, local copies, waits for them, and re-layouts: 8.82 us -> 1.54 us
    pallas_call x1, Pallas kernels: 50.2 us -> 45.6 us  [shards(): pl.pallas_call(kernel, out_shape=jax.ShapeDtypeStruct(tokens.shape, token...]
    reshape x5 -> x0, local copies, waits for them, and re-layouts: 3.43 us -> none  [the longest x1 0.69 us: shards(): conv_bias.reshape(1, -1)]
where the time goes in v2:
time: 47.3 us; the launch traced here: 47.2 us
  Pallas kernels  45.6 us (96%)
  local copies, waits for them, and re-layouts  1.54 us (3%)
    pallas_call x1, Pallas kernels, shards(): pl.pallas_call(kernel, out_shape=jax.ShapeDtypeStruct(tokens.shape, token...  45.6 us
    unnamed x1, local copies, waits for them, and re-layouts  1.54 us

profile of v2, /device:TPU:1, one launch (start us, length us, event | category | flops | bytes accessed | tf_op | source)
XLA Modules:
  0.0 47.2 jit_solution(18434659952333160278)
XLA Ops:
  0.0 45.6 %shard_map.136 = bf16[8,16,384]{2,1,0:T(8,128)(2,1)} custom-call(bf16[8,16,384]{2,1,0:T(8,128)(2,1)} %tokens_hbm.1, bf16[384,1536]{1,0:T(8,128)(2,1)} %w_in_hbm.1, f32[384]{0:T(512)} %norm_gain_hbm.1, f32[384]{0:T(512)} %norm_bias_hbm.1, f32[9,768]{1,0:T(8,128)} %taps_hbm.1, f32[768]{0:T(1024)} %conv_bias_hbm.1, bf16[160,768]{1,0:T(8,128)(2,1)} %bitcast.4, ...), custom_call_target="tpu_custom_call" | custom-call | tf_op jit(solution)/shard_map/pallas_call | solution.py:392
  45.6 1.5 %copy.16 = bf16[8,16,384]{2,1,0:T(8,128)(2,1)} copy(bf16[8,16,384]{2,1,0:T(8,128)(2,1)} %shard_map.136) | data formatting | bytes 196608

commit v3 on v2

--- a/solution.py
+++ b/solution.py
@@ -41,7 +41,7 @@
     out,
     tokens, w_in, norm_gain, norm_bias, taps, conv_bias, w_xt, w_dt, dt_bias, a_log, d_skip, out_gain, out_bias, w_out,
     load_sem,
-    edge, edge_row, edge_col, halo, padded, conved, summed, gate, row_out, col_out, row_in, col_in,
+    edge, edge_row, edge_col, halo, padded, beside, conved, summed, gate, row_out, col_out, row_in, col_in,
     cell_maps, steps, drive, in_map, out_map, row_sum, col_sum, state_out, state_in,
     row_back_out, col_back_out, row_back_in, col_back_in,
     edge_send, edge_recv, row_send, row_recv, col_send, col_recv, state_send, state_recv,
@@ -71,8 +71,7 @@
         (d_skip_hbm, d_skip), (out_gain_hbm, out_gain), (out_bias_hbm, out_bias), (w_out_hbm, w_out),
     ]
     loads = [pltpu.make_async_copy(src, dst, load_sem.at[i]) for i, (src, dst) in enumerate(pairs)]
-    for item in loads:
-        item.start()
+    loads[0].start()
 
     barrier = pltpu.get_barrier_semaphore()
 
@@ -92,6 +91,8 @@
 
     lax.fori_loop(1, ROWS, greet_row, 0)
     lax.fori_loop(own_col, COLS, greet_col, 0)
+    for item in loads[1:]:
+        item.start()
 
     def copy(src, dst, send, recv, device):
         return pltpu.make_async_remote_copy(
@@ -111,10 +112,10 @@
         (edge_row.at[1], halo.at[0], 0, around[1]),
         (edge_col.at[0], edge.at[1], 3, around[2]),
         (edge_col.at[1], edge.at[0], 2, around[3]),
-        (edge_col.at[0], edge.at[5], 7, around[4]),
-        (edge_col.at[1], edge.at[4], 6, around[5]),
-        (edge_col.at[0], edge.at[3], 5, around[6]),
-        (edge_col.at[1], edge.at[2], 4, around[7]),
+        (edge_col.at[0, pl.ds(0, 1)], edge.at[5, pl.ds(0, 1)], 7, around[4]),
+        (edge_col.at[1, pl.ds(0, 1)], edge.at[4, pl.ds(0, 1)], 6, around[5]),
+        (edge_col.at[0, pl.ds(7, 1)], edge.at[3, pl.ds(7, 1)], 5, around[6]),
+        (edge_col.at[1, pl.ds(7, 1)], edge.at[2, pl.ds(7, 1)], 4, around[7]),
     ]
     edges = [copy(src, dst, edge_send.at[slot], edge_recv.at[slot], device) for src, dst, slot, device in sends]
     for item in edges:
@@ -133,15 +134,27 @@
     width = gate.shape[1]
     hw, groups = width // 2, width // LANES
     inner = rounded(jnp.dot(normed, w_in[:, :width], preferred_element_type=F32))
+    padded[...] = jnp.zeros(padded.shape, F32)
     padded[1 : 1 + ROWS, 8 : 8 + COLS, :] = inner.reshape(ROWS, COLS, width)
-    gate[...] = rounded(jnp.dot(normed, w_in[:, width:], preferred_element_type=F32))
-
+    gate[...] = silu(rounded(jnp.dot(normed, w_in[:, width:], preferred_element_type=F32)))
+
+    def conv_row(r, carry):
+        total = jnp.broadcast_to(conv_bias[...].reshape(1, -1), (COLS, width))
+        for i in range(3):
+            for j in range(3):
+                tap = 3 * i + j
+                total = total + padded[r + i, 7 + j : 7 + j + COLS, :] * taps[tap : tap + 1, :]
+        for g in range(groups):
+            conved[g, pl.ds(pl.multiple_of(r * COLS, COLS), COLS), :] = total[:, g * LANES : (g + 1) * LANES]
+        return carry
+
+    lax.fori_loop(0, ROWS, conv_row, 0)
     for item in edges:
         item.wait_recv()
     rim = jnp.concatenate(
         [
             halo[0].astype(F32), halo[1].astype(F32), edge[0], edge[1],
-            edge[2, 7:8, :], edge[3, 7:8, :], edge[4, 0:1, :], edge[5, 0:1, :], edge[2, 0:4, :],
+            edge[2, 7:8, :], edge[3, 7:8, :], edge[4, 0:1, :], edge[5, 0:1, :], edge[0, 0:4, :],
         ],
         axis=0,
     )
@@ -150,15 +163,28 @@
     has_s = (my_y < ny - 1).astype(F32)
     has_w = (my_x > 0).astype(F32)
     has_e = (my_x < nx - 1).astype(F32)
-    padded[0, 8 : 8 + COLS, :] = rim[0:16] * has_n
-    padded[1 + ROWS, 8 : 8 + COLS, :] = rim[16:32] * has_s
-    for r in range(ROWS):
-        padded[1 + r, 7:8, :] = rim[32 + r : 33 + r] * has_w
-        padded[1 + r, 8 + COLS : 9 + COLS, :] = rim[40 + r : 41 + r] * has_e
-    padded[0, 7:8, :] = rim[48:49] * (has_n * has_w)
-    padded[0, 8 + COLS : 9 + COLS, :] = rim[49:50] * (has_n * has_e)
-    padded[1 + ROWS, 7:8, :] = rim[50:51] * (has_s * has_w)
-    padded[1 + ROWS, 8 + COLS : 9 + COLS, :] = rim[51:52] * (has_s * has_e)
+    beside[0, 8 : 8 + COLS, :] = rim[0:16] * has_n
+    beside[0, 7:8, :] = rim[48:49] * (has_n * has_w)
+    beside[0, 8 + COLS : 9 + COLS, :] = rim[49:50] * (has_n * has_e)
+    beside[1, 8 : 8 + COLS, :] = rim[16:32] * has_s
+    beside[1, 7:8, :] = rim[50:51] * (has_s * has_w)
+    beside[1, 8 + COLS : 9 + COLS, :] = rim[51:52] * (has_s * has_e)
+    nothing = jnp.zeros((8, width), F32)
+    for side, value in ((2, rim[32:40] * has_w), (3, rim[40:48] * has_e)):
+        beside[side, 0:8, :] = nothing
+        beside[side, 8:16, :] = value
+        beside[side, 16:24, :] = nothing
+    for side, row in ((0, 0), (1, ROWS - 1)):
+        more = sum(beside[side, 7 + j : 7 + j + COLS, :] * taps[6 * side + j : 6 * side + j + 1, :] for j in range(3))
+        for g in range(groups):
+            here = (g, slice(row * COLS, row * COLS + COLS))
+            conved[here] = conved[here] + more[:, g * LANES : (g + 1) * LANES]
+    for side, col in ((2, 0), (3, COLS - 1)):
+        tap = 0 if side == 2 else 2
+        more = sum(beside[side, 7 + i : 15 + i, :] * taps[3 * i + tap : 3 * i + tap + 1, :] for i in range(3))
+        for g in range(groups):
+            here = (g, pl.ds(col, ROWS, stride=COLS))
+            conved[here] = conved[here] + more[:, g * LANES : (g + 1) * LANES]
 
     def row_copy(member):
         return copy(row_out.at[member], row_in.at[member_x], row_send.at[member], row_recv.at[member_x], in_row(member))
@@ -166,40 +192,37 @@
     def col_copy(member):
         return copy(col_out.at[member], col_in.at[member_y], col_send.at[member], col_recv.at[member_y], in_col(member))
 
-    def conv_row(r, carry):
-        total = jnp.broadcast_to(conv_bias[...].reshape(1, -1), (COLS, width))
-        for i in range(3):
-            for j in range(3):
-                tap = 3 * i + j
-                total = total + padded[r + i, 7 + j : 7 + j + COLS, :] * taps[tap : tap + 1, :]
-        value = silu(total).astype(BF16)
-        row_out[r] = value
+    for r in range(ROWS):
         for g in range(groups):
-            conved[g, pl.ds(pl.multiple_of(r * COLS, COLS), COLS), :] = value[:, g * LANES : (g + 1) * LANES].astype(F32)
-
-        @pl.when(r != member_x)
-        def _():
-            row_copy(r).start()
-
-        return carry
-
-    lax.fori_loop(0, ROWS, conv_row, 0)
-    row_in[member_x] = row_out[member_x]
+            here = (g, slice(r * COLS, r * COLS + COLS))
+            value = silu(conved[here]).astype(BF16)
+            row_out[r, :, g * LANES : (g + 1) * LANES] = value
+            conved[here] = value.astype(F32)
     for c in range(COLS):
         column = [conved[g, pl.ds(c, ROWS, stride=COLS), :] for g in range(groups)]
         for g in range(groups // 2):
             both = jnp.concatenate([column[g], column[g + groups // 2]], axis=0)
             col_out[c, :, g * LANES : (g + 1) * LANES] = both.astype(BF16)
 
+    def start_col(turn, carry):
+        col_copy(lax.rem(member_y + turn, COLS)).start()
+        return carry
+
+    def start_row(turn, carry):
+        row_copy(lax.rem(member_x + turn, ROWS)).start()
+        return carry
+
+    lax.fori_loop(own_col, COLS, start_col, 0)
+    lax.fori_loop(1, ROWS, start_row, 0)
+    row_in[member_x] = row_out[member_x]
+
     @pl.when(own_col == 1)
     def _():
         col_in[member_y] = col_out[member_y]
 
-    def start_col(turn, carry):
-        col_copy(lax.rem(member_y + turn, COLS)).start()
-        return carry
-
-    lax.fori_loop(own_col, COLS, start_col, 0)
+    skip = jnp.sum(d_skip[...], axis=0, keepdims=True)
+    for g in range(groups):
+        summed[g, :LINE] = skip[:, g * LANES : (g + 1) * LANES] * conved[g, :LINE]
 
     def split_columns(stacked):
         value = stacked.astype(F32)
@@ -240,7 +263,7 @@
 
     sub = lax.broadcasted_iota(jnp.int32, (8, LANES), 0)
 
-    def scan(k, backward, start, total, first):
+    def scan(k, backward, start, total, first, finish=None):
         rates = -jnp.exp(a_log[k]) * LOG2E
         masks = [lax.rem(sub // s, 2) == backward for s in (1, 2, 4)]
 
@@ -248,7 +271,7 @@
             base = pl.multiple_of((turn + backward * (LINE // 8 - 1 - 2 * turn)) * 8, 8)
             cell = [base + i + backward * (7 - 2 * i) for i in range(8)]
             state = list(state)
-            for g in range(width // LANES):
+            for g in range(groups):
                 lanes = slice(g * LANES, (g + 1) * LANES)
                 parts = []
                 for i in range(8):
@@ -265,7 +288,13 @@
                 total[here] = parts[0] if first else total[here] + parts[0]
             return tuple(state)
 
-        return lax.fori_loop(0, LINE // 8, chunk, start)
+        def pair(turn, state):
+            state = chunk(2 * turn + 1, chunk(2 * turn, state))
+            if finish is not None:
+                finish(turn + backward * (LINE // 16 - 1 - 2 * turn))
+            return state
+
+        return lax.fori_loop(0, LINE // 16, pair, start)
 
     def split(state):
         return tuple(state[:, g * LANES : (g + 1) * LANES] for g in range(width // LANES))
@@ -301,38 +330,38 @@
     prepare(col_cells, 2)
     send_state(1, scan(2 + half_y, half_y, zero, col_sum, True))
 
-    state_copies[0].wait_recv()
-    scan(1 - half_x, 1 - half_x, split(state_in[0]), row_sum, False)
-    row_back_out[...] = row_sum[...].astype(BF16).reshape(ROWS, COLS, width)
-    row_back_in[member_x] = row_back_out[member_x]
-
     def row_back(member, slot):
         return copy(row_back_out.at[member], row_back_in.at[slot], row_back_send.at[member], row_back_recv.at[slot], in_row(member))
 
     def col_back(member, slot):
         return copy(col_back_out.at[member], col_back_in.at[slot], col_back_send.at[member], col_back_recv.at[slot], in_col(member))
 
-    def start_row_back(turn, carry):
-        row_back(lax.rem(member_x + turn, ROWS), member_x).start()
-        return carry
-
-    lax.fori_loop(1, ROWS, start_row_back, 0)
+    def finish_row(member):
+        row_back_out[member] = row_sum[pl.ds(pl.multiple_of(member * COLS, COLS), COLS), :].astype(BF16)
+
+        @pl.when(member != member_x)
+        def _():
+            row_back(member, member_x).start()
+
+    def finish_col(two):
+        for member in (2 * two, 2 * two + 1):
+            value = col_sum[pl.ds(pl.multiple_of(member * ROWS, ROWS), ROWS), :]
+            col_back_out[member] = jnp.concatenate([value[:, :hw], value[:, hw:]], axis=0).astype(BF16)
+
+            @pl.when((member != member_y) | (own_col == 0))
+            def _():
+                col_back(member, member_y).start()
 
     state_copies[1].wait_recv()
-    scan(3 - half_y, 1 - half_y, split(state_in[1]), col_sum, False)
-    col_value = col_sum[...].reshape(COLS, ROWS, width)
-    col_back_out[...] = jnp.concatenate([col_value[:, :, :hw], col_value[:, :, hw:]], axis=1).astype(BF16)
+    scan(3 - half_y, 1 - half_y, split(state_in[1]), col_sum, False, finish_col)
+    state_copies[0].wait_recv()
+    scan(1 - half_x, 1 - half_x, split(state_in[0]), row_sum, False, finish_row)
+    row_back_in[member_x] = row_back_out[member_x]
 
     @pl.when(own_col == 1)
     def _():
         col_back_in[member_y] = col_back_out[member_y]
 
-    def start_col_back(turn, carry):
-        col_back(lax.rem(member_y + turn, COLS), member_y).start()
-        return carry
-
-    lax.fori_loop(own_col, COLS, start_col_back, 0)
-
     def wait_row_back(turn, carry):
         member = lax.rem(member_x + turn, ROWS)
         row_back(member, member).wait_recv()
@@ -344,11 +373,9 @@
         return carry
 
     lax.fori_loop(1, ROWS, wait_row_back, 0)
-    skip = jnp.sum(d_skip[...], axis=0, keepdims=True)
     row_value = row_back_in[...].reshape(LINE, width).astype(F32)
     for g in range(groups):
-        lanes = slice(g * LANES, (g + 1) * LANES)
-        summed[g, :LINE] = row_value[:, lanes] + skip[:, lanes] * conved[g, :LINE]
+        summed[g, :LINE] = summed[g, :LINE] + row_value[:, g * LANES : (g + 1) * LANES]
     lax.fori_loop(own_col, COLS, wait_col_back, 0)
     for c in range(COLS):
         value = col_back_in[c].astype(F32)
@@ -358,7 +385,7 @@
             lane = (g % (groups // 2)) * LANES
             summed[here] = summed[here] + value[low:high, lane : lane + LANES]
     total = jnp.concatenate([summed[g, :LINE] for g in range(groups)], axis=1)
-    gated = (unit_norm(total) * out_gain[...].reshape(1, -1) + out_bias[...].reshape(1, -1)) * silu(gate[...])
+    gated = (unit_norm(total) * out_gain[...].reshape(1, -1) + out_bias[...].reshape(1, -1)) * gate[...]
     mixed = tokens[...].astype(F32).reshape(ROWS * COLS, -1) + jnp.dot(gated.astype(BF16), w_out[...], preferred_element_type=F32)
     out[...] = mixed.reshape(out.shape).astype(BF16)
 
@@ -401,6 +428,7 @@
             pltpu.VMEM((2, ROWS, chans), F32),
             pltpu.VMEM((2, COLS, chans), BF16),
             pltpu.VMEM((ROWS + 2, COLS + 16, width), F32),
+            pltpu.VMEM((4, COLS + 16, width), F32),
             pltpu.VMEM((width // LANES, LINE + COLS, LANES), F32),
             pltpu.VMEM((width // LANES, LINE + COLS, LANES), F32),
             pltpu.VMEM((ROWS * COLS, width), F32),

time: 47.3 us -> 44.1 us (0.932)
  Pallas kernels: 45.6 us -> 42.4 us
    pallas_call x1, Pallas kernels: 45.6 us -> 42.4 us  [shards(): pl.pallas_call(kernel, out_shape=jax.ShapeDtypeStruct(tokens.shape, token...]
where the time goes in v3:
time: 44.1 us; the launch traced here: 44 us
  Pallas kernels  42.4 us (96%)
  local copies, waits for them, and re-layouts  1.54 us (3%)
    pallas_call x1, Pallas kernels, shards(): pl.pallas_call(kernel, out_shape=jax.ShapeDtypeStruct(tokens.shape, token...  42.4 us
    unnamed x1, local copies, waits for them, and re-layouts  1.54 us

profile of v3, /device:TPU:1, one launch (start us, length us, event | category | flops | bytes accessed | tf_op | source)
XLA Modules:
  0.0 44.0 jit_solution(3635858488087140322)
XLA Ops:
  0.0 42.4 %shard_map.136 = bf16[8,16,384]{2,1,0:T(8,128)(2,1)} custom-call(bf16[8,16,384]{2,1,0:T(8,128)(2,1)} %tokens_hbm.1, bf16[384,1536]{1,0:T(8,128)(2,1)} %w_in_hbm.1, f32[384]{0:T(512)} %norm_gain_hbm.1, f32[384]{0:T(512)} %norm_bias_hbm.1, f32[9,768]{1,0:T(8,128)} %taps_hbm.1, f32[768]{0:T(1024)} %conv_bias_hbm.1, bf16[160,768]{1,0:T(8,128)(2,1)} %bitcast.4, ...), custom_call_target="tpu_custom_call" | custom-call | tf_op jit(solution)/shard_map/pallas_call | solution.py:419
  42.4 1.5 %copy.16 = bf16[8,16,384]{2,1,0:T(8,128)(2,1)} copy(bf16[8,16,384]{2,1,0:T(8,128)(2,1)} %shard_map.136) | data formatting | bytes 196608

commit v4 on v3

--- a/solution.py
+++ b/solution.py
@@ -42,7 +42,7 @@
     tokens, w_in, norm_gain, norm_bias, taps, conv_bias, w_xt, w_dt, dt_bias, a_log, d_skip, out_gain, out_bias, w_out,
     load_sem,
     edge, edge_row, edge_col, halo, padded, beside, conved, summed, gate, row_out, col_out, row_in, col_in,
-    cell_maps, steps, drive, in_map, out_map, row_sum, col_sum, state_out, state_in,
+    cell_maps, spread, steps, drive, in_map, out_map, row_sum, col_sum, state_out, state_in,
     row_back_out, col_back_out, row_back_in, col_back_in,
     edge_send, edge_recv, row_send, row_recv, col_send, col_recv, state_send, state_recv,
     row_back_send, row_back_recv, col_back_send, col_back_recv,
@@ -186,11 +186,23 @@
             here = (g, pl.ds(col, ROWS, stride=COLS))
             conved[here] = conved[here] + more[:, g * LANES : (g + 1) * LANES]
 
+    def settle_rows(src, dst, send, recv, what):
+        item = copy(src.at[pl.ds(0, ROWS - 1)], dst.at[pl.ds(0, ROWS - 1)], send.at[0], recv.at[0], over_x)
+        getattr(item, what)()
+
+    def settle_cols(src, dst, send, recv, what):
+        for own in range(2):
+
+            @pl.when(own_col == own)
+            def _(own=own):
+                here = pl.ds(0, COLS - own)
+                getattr(copy(src.at[here], dst.at[here], send.at[0], recv.at[0], over_y), what)()
+
     def row_copy(member):
-        return copy(row_out.at[member], row_in.at[member_x], row_send.at[member], row_recv.at[member_x], in_row(member))
+        return copy(row_out.at[member], row_in.at[member_x], row_send.at[0], row_recv.at[0], in_row(member))
 
     def col_copy(member):
-        return copy(col_out.at[member], col_in.at[member_y], col_send.at[member], col_recv.at[member_y], in_col(member))
+        return copy(col_out.at[member], col_in.at[member_y], col_send.at[0], col_recv.at[0], in_col(member))
 
     for r in range(ROWS):
         for g in range(groups):
@@ -235,31 +247,34 @@
     lane = lax.broadcasted_iota(jnp.int32, (8, LANES), 1)
     own_state = lane % 8 == lax.broadcasted_iota(jnp.int32, (8, LANES), 0)
 
-    def prepare(cells, first):
-        weight = w_xt[40 * first : 40 * first + 80, :]
+    def project_maps(cells, line):
+        weight = w_xt[80 * line : 80 * line + 80, :]
         proj = lax.dot_general(cells, weight, (((1,), (1,)), ((), ())), preferred_element_type=F32)
-        cells_float = cells.astype(F32)
-        ranks = w_dt[...].astype(F32)
-        for side in range(2):
-            k = first + side
-            low = proj[:, 40 * side : 40 * side + 24].astype(BF16)
-            rank = ranks[24 * k : 24 * k + 24].astype(BF16)
-            step = softplus(jnp.dot(low, rank, preferred_element_type=F32) + dt_bias[k : k + 1, :])
-            push = step * cells_float
-            for g in range(groups):
-                steps[k, g, :LINE] = step[:, g * LANES : (g + 1) * LANES]
-                drive[k, g, :LINE] = push[:, g * LANES : (g + 1) * LANES]
         proj = jnp.concatenate([proj, jnp.zeros((LINE, LANES - 80), F32)], axis=1)
         high = rounded(proj)
         left = rounded(proj - high)
         wide = lax.broadcasted_iota(jnp.int32, (LINE, LANES), 1)
-        cell_maps[:LINE] = jnp.where(wide < 80, high, jnp.where(wide < 96, pltpu.roll(left, 56, 1), pltpu.roll(left, 32, 1)))
-        rows = [jnp.where(own_state, cell_maps[pl.ds(cell, 8, stride=0), :], 0.0) for cell in range(LINE)]
-        maps = jnp.dot(jnp.concatenate(rows, axis=0).astype(BF16), pick, preferred_element_type=F32)
-        maps = maps.reshape(LINE, 8, 4 * LANES)
-        for side in range(2):
-            in_map[first + side] = maps[:, :, 2 * side * LANES : (2 * side + 1) * LANES]
-            out_map[first + side] = maps[:, :, (2 * side + 1) * LANES : (2 * side + 2) * LANES]
+        cell_maps[line, :LINE] = jnp.where(wide < 80, high, jnp.where(wide < 96, pltpu.roll(left, 56, 1), pltpu.roll(left, 32, 1)))
+        rows = [jnp.where(own_state, cell_maps[line, pl.ds(cell, 8, stride=0), :], 0.0) for cell in range(LINE)]
+        spread[line] = jnp.concatenate(rows, axis=0).astype(BF16)
+
+    def prepare(cells, line, side):
+        k = 2 * line + side
+        first = side == 0
+        low = cell_maps[line, :LINE]
+        low = jnp.where(first, low[:, 0:24], low[:, 40:64]).astype(BF16)
+        ranks = w_dt[48 * line : 48 * line + 48, :].astype(F32)
+        rank = jnp.where(first, ranks[0:24], ranks[24:48]).astype(BF16)
+        offset = jnp.where(first, dt_bias[2 * line : 2 * line + 1, :], dt_bias[2 * line + 1 : 2 * line + 2, :])
+        step = softplus(jnp.dot(low, rank, preferred_element_type=F32) + offset)
+        push = step * cells.astype(F32)
+        for g in range(groups):
+            steps[k, g, :LINE] = step[:, g * LANES : (g + 1) * LANES]
+            drive[k, g, :LINE] = push[:, g * LANES : (g + 1) * LANES]
+        wanted = jnp.where(first, pick[:, : 2 * LANES], pick[:, 2 * LANES :])
+        maps = jnp.dot(spread[line], wanted, preferred_element_type=F32).reshape(LINE, 8, 2 * LANES)
+        in_map[k] = maps[:, :, :LANES]
+        out_map[k] = maps[:, :, LANES:]
 
     sub = lax.broadcasted_iota(jnp.int32, (8, LANES), 0)
 
@@ -305,36 +320,28 @@
         copy(state_out.at[1], state_in.at[1], state_send.at[1], state_recv.at[1], over_y),
     ]
 
-    def wait_row(turn, carry):
-        member = lax.rem(member_x + turn, ROWS)
-        copy(row_out.at[member], row_in.at[member], row_send.at[member], row_recv.at[member], in_row(member)).wait_recv()
-        return carry
-
-    def wait_col(turn, carry):
-        member = lax.rem(member_y + turn, COLS)
-        copy(col_out.at[member], col_in.at[member], col_send.at[member], col_recv.at[member], in_col(member)).wait_recv()
-        return carry
-
     def send_state(index, state):
         for g in range(width // LANES):
             state_out[index, :, g * LANES : (g + 1) * LANES] = state[g]
         state_copies[index].start()
 
-    lax.fori_loop(1, ROWS, wait_row, 0)
+    settle_rows(row_out, row_in, row_send, row_recv, "wait_recv")
     row_cells = row_in[...].reshape(LINE, width)
-    prepare(row_cells, 0)
+    project_maps(row_cells, 0)
+    prepare(row_cells, 0, half_x)
     send_state(0, scan(half_x, half_x, zero, row_sum, True))
 
-    lax.fori_loop(own_col, COLS, wait_col, 0)
+    settle_cols(col_out, col_in, col_send, col_recv, "wait_recv")
     col_cells = split_columns(col_in[...]).astype(BF16)
-    prepare(col_cells, 2)
+    project_maps(col_cells, 1)
+    prepare(col_cells, 1, half_y)
     send_state(1, scan(2 + half_y, half_y, zero, col_sum, True))
 
     def row_back(member, slot):
-        return copy(row_back_out.at[member], row_back_in.at[slot], row_back_send.at[member], row_back_recv.at[slot], in_row(member))
+        return copy(row_back_out.at[member], row_back_in.at[slot], row_back_send.at[0], row_back_recv.at[0], in_row(member))
 
     def col_back(member, slot):
-        return copy(col_back_out.at[member], col_back_in.at[slot], col_back_send.at[member], col_back_recv.at[slot], in_col(member))
+        return copy(col_back_out.at[member], col_back_in.at[slot], col_back_send.at[0], col_back_recv.at[0], in_col(member))
 
     def finish_row(member):
         row_back_out[member] = row_sum[pl.ds(pl.multiple_of(member * COLS, COLS), COLS), :].astype(BF16)
@@ -352,8 +359,10 @@
             def _():
                 col_back(member, member_y).start()
 
+    prepare(col_cells, 1, 1 - half_y)
     state_copies[1].wait_recv()
     scan(3 - half_y, 1 - half_y, split(state_in[1]), col_sum, False, finish_col)
+    prepare(row_in[...].reshape(LINE, width), 0, 1 - half_x)
     state_copies[0].wait_recv()
     scan(1 - half_x, 1 - half_x, split(state_in[0]), row_sum, False, finish_row)
     row_back_in[member_x] = row_back_out[member_x]
@@ -362,21 +371,17 @@
     def _():
         col_back_in[member_y] = col_back_out[member_y]
 
-    def wait_row_back(turn, carry):
-        member = lax.rem(member_x + turn, ROWS)
-        row_back(member, member).wait_recv()
-        return carry
-
-    def wait_col_back(turn, carry):
-        member = lax.rem(member_y + turn, COLS)
-        col_back(member, member).wait_recv()
-        return carry
-
-    lax.fori_loop(1, ROWS, wait_row_back, 0)
+    for item in edges + state_copies:
+        item.wait_send()
+    settle_rows(row_out, row_in, row_send, row_recv, "wait_send")
+    settle_cols(col_out, col_in, col_send, col_recv, "wait_send")
+    settle_rows(row_back_out, row_back_in, row_back_send, row_back_recv, "wait_recv")
     row_value = row_back_in[...].reshape(LINE, width).astype(F32)
     for g in range(groups):
         summed[g, :LINE] = summed[g, :LINE] + row_value[:, g * LANES : (g + 1) * LANES]
-    lax.fori_loop(own_col, COLS, wait_col_back, 0)
+    settle_cols(col_back_out, col_back_in, col_back_send, col_back_recv, "wait_send")
+    settle_rows(row_back_out, row_back_in, row_back_send, row_back_recv, "wait_send")
+    settle_cols(col_back_out, col_back_in, col_back_send, col_back_recv, "wait_recv")
     for c in range(COLS):
         value = col_back_in[c].astype(F32)
         for g in range(groups):
@@ -388,24 +393,6 @@
     gated = (unit_norm(total) * out_gain[...].reshape(1, -1) + out_bias[...].reshape(1, -1)) * gate[...]
     mixed = tokens[...].astype(F32).reshape(ROWS * COLS, -1) + jnp.dot(gated.astype(BF16), w_out[...], preferred_element_type=F32)
     out[...] = mixed.reshape(out.shape).astype(BF16)
-
-    for item in edges + state_copies:
-        item.wait_send()
-
-    def drain_row(turn, carry):
-        member = lax.rem(member_x + turn, ROWS)
-        row_copy(member).wait_send()
-        row_back(member, member_x).wait_send()
-        return carry
-
-    def drain_col(turn, carry):
-        member = lax.rem(member_y + turn, COLS)
-        col_copy(member).wait_send()
-        col_back(member, member_y).wait_send()
-        return carry
-
-    lax.fori_loop(1, ROWS, drain_row, 0)
-    lax.fori_loop(own_col, COLS, drain_col, 0)
 
 
 def shards(tokens, norm_gain, norm_bias, w_in, conv_taps, conv_bias, w_x, w_dt, dt_bias, a_log, d_skip, out_gain, out_bias, w_out):
@@ -436,7 +423,8 @@
             pltpu.VMEM((COLS, 2 * ROWS, hw), BF16),
             pltpu.VMEM((ROWS, COLS, width), BF16),
             pltpu.VMEM((COLS, 2 * ROWS, hw), BF16),
-            pltpu.VMEM((LINE + 8, LANES), F32),
+            pltpu.VMEM((2, LINE + 8, LANES), F32),
+            pltpu.VMEM((2, LINE * 8, LANES), BF16),
             pltpu.VMEM((4, width // LANES, LINE + 8, LANES), F32),
             pltpu.VMEM((4, width // LANES, LINE + 8, LANES), F32),
             pltpu.VMEM((4, LINE, 8, LANES), F32),
@@ -449,8 +437,8 @@
             pltpu.VMEM((COLS, 2 * ROWS, hw), BF16),
             pltpu.VMEM((ROWS, COLS, width), BF16),
             pltpu.VMEM((COLS, 2 * ROWS, hw), BF16),
-            dma((8,)), dma((8,)), dma((ROWS,)), dma((ROWS,)), dma((COLS,)), dma((COLS,)), dma((2,)), dma((2,)),
-            dma((ROWS,)), dma((ROWS,)), dma((COLS,)), dma((COLS,)),
+            dma((8,)), dma((8,)), dma((1,)), dma((1,)), dma((1,)), dma((1,)), dma((2,)), dma((2,)),
+            dma((1,)), dma((1,)), dma((1,)), dma((1,)),
         ],
         compiler_params=pltpu.CompilerParams(collective_id=0, has_side_effects=True, vmem_limit_bytes=60 * 1024 * 1024),
     )(*operands)

time: 44.1 us -> 42.3 us (0.959)
  Pallas kernels: 42.4 us -> 40.6 us
    pallas_call x1, Pallas kernels: 42.4 us -> 40.6 us  [shards(): pl.pallas_call(kernel, out_shape=jax.ShapeDtypeStruct(tokens.shape, token...]
where the time goes in v4:
time: 42.3 us; the launch traced here: 42.2 us
  Pallas kernels  40.6 us (96%)
  local copies, waits for them, and re-layouts  1.54 us (4%)
    pallas_call x1, Pallas kernels, shards(): pl.pallas_call(kernel, out_shape=jax.ShapeDtypeStruct(tokens.shape, token...  40.6 us
    unnamed x1, local copies, waits for them, and re-layouts  1.54 us

profile of v4, /device:TPU:1, one launch (start us, length us, event | category | flops | bytes accessed | tf_op | source)
XLA Modules:
  0.0 42.2 jit_solution(18131893426351160995)
XLA Ops:
  0.0 40.6 %shard_map.136 = bf16[8,16,384]{2,1,0:T(8,128)(2,1)} custom-call(bf16[8,16,384]{2,1,0:T(8,128)(2,1)} %tokens_hbm.1, bf16[384,1536]{1,0:T(8,128)(2,1)} %w_in_hbm.1, f32[384]{0:T(512)} %norm_gain_hbm.1, f32[384]{0:T(512)} %norm_bias_hbm.1, f32[9,768]{1,0:T(8,128)} %taps_hbm.1, f32[768]{0:T(1024)} %conv_bias_hbm.1, bf16[160,768]{1,0:T(8,128)(2,1)} %bitcast.4, ...), custom_call_target="tpu_custom_call" | custom-call | tf_op jit(solution)/shard_map/pallas_call | solution.py:406
  40.6 1.5 %copy.16 = bf16[8,16,384]{2,1,0:T(8,128)(2,1)} copy(bf16[8,16,384]{2,1,0:T(8,128)(2,1)} %shard_map.136) | data formatting | bytes 196608

commit v5 on v4

--- a/solution.py
+++ b/solution.py
@@ -89,8 +89,15 @@
         greet(in_col(lax.rem(member_y + turn, COLS)))
         return carry
 
-    lax.fori_loop(1, ROWS, greet_row, 0)
-    lax.fori_loop(own_col, COLS, greet_col, 0)
+    for turn in range(1, COLS):
+        greet_col(turn, 0)
+
+    @pl.when(own_col == 0)
+    def _():
+        greet_col(0, 0)
+
+    for turn in range(1, ROWS):
+        greet_row(turn, 0)
     for item in loads[1:]:
         item.start()
 
@@ -224,8 +231,15 @@
         row_copy(lax.rem(member_x + turn, ROWS)).start()
         return carry
 
-    lax.fori_loop(own_col, COLS, start_col, 0)
-    lax.fori_loop(1, ROWS, start_row, 0)
+    for turn in range(1, COLS):
+        start_col(turn, 0)
+
+    @pl.when(own_col == 0)
+    def _():
+        start_col(0, 0)
+
+    for turn in range(1, ROWS):
+        start_row(turn, 0)
     row_in[member_x] = row_out[member_x]
 
     @pl.when(own_col == 1)

time: 42.3 us -> 42.2 us (level)
  no operation moved by 1% of the time
where the time goes in v5:
time: 42.2 us; the launch traced here: 42 us
  Pallas kernels  40.5 us (96%)
  local copies, waits for them, and re-layouts  1.54 us (4%)
    pallas_call x1, Pallas kernels, shards(): pl.pallas_call(kernel, out_shape=jax.ShapeDtypeStruct(tokens.shape, token...  40.5 us
    unnamed x1, local copies, waits for them, and re-layouts  1.54 us

profile of v5, /device:TPU:1, one launch (start us, length us, event | category | flops | bytes accessed | tf_op | source)
XLA Modules:
  0.0 42.0 jit_solution(2669759368205754957)
XLA Ops:
  0.0 40.5 %shard_map.136 = bf16[8,16,384]{2,1,0:T(8,128)(2,1)} custom-call(bf16[8,16,384]{2,1,0:T(8,128)(2,1)} %tokens_hbm.1, bf16[384,1536]{1,0:T(8,128)(2,1)} %w_in_hbm.1, f32[384]{0:T(512)} %norm_gain_hbm.1, f32[384]{0:T(512)} %norm_bias_hbm.1, f32[9,768]{1,0:T(8,128)} %taps_hbm.1, f32[768]{0:T(1024)} %conv_bias_hbm.1, bf16[160,768]{1,0:T(8,128)(2,1)} %bitcast.4, ...), custom_call_target="tpu_custom_call" | custom-call | tf_op jit(solution)/shard_map/pallas_call | solution.py:420
  40.5 1.5 %copy.16 = bf16[8,16,384]{2,1,0:T(8,128)(2,1)} copy(bf16[8,16,384]{2,1,0:T(8,128)(2,1)} %shard_map.136) | data formatting | bytes 196608
